TPU v7x, 256 devices: a whole 4x4x8 slice. The times are simulated.
256 devices in a mesh: ia: 8 (over z_hi, x), ja: 32 (over y, z_lo, core).
Axes of the slice: x: 4, y: 4, z: 8 (z_hi: 2, z_lo: 4; z = z_hi * 4 + z_lo), core: 2. Of those that a mesh axis runs over, the one named last changes fastest.
Arguments:
- amplitudes: float32 [64, 64, 8192], P('ia', 'ja'), may hold values from -6 to 6
- residual_in: float32 [64, 64, 8192], P('ia', 'ja'), may hold values from -6 to 6
- ladder_ints: float32 [8192, 8192], P('ja'), may hold values from -0.0625 to 0.0625
- occ_energy: float32 [64], replicated, may hold values from -3 to -0.5
- virt_energy: float32 [256], replicated, may hold values from 0.3 to 3
- virt_order: int32 [256], replicated, may hold values from 0 to 255, each once
Outputs:
- residual: float32 [64, 64, 8192], P('ia', 'ja')
- new_amplitudes: float32 [64, 64, 8192], P('ia', 'ja')
Inputs may be any that keep to these rules, and one draw needn't show every extreme that they name: `virt_order`: each orbital number appears once; entries h * 32 to (h + 1) * 32 - 1 are the virtuals of irrep h.
All inputs are finite; a program needn't handle non-finite values.
Results may differ from a plain program's by a relative error of at most 0.000059.
Values sent between devices are 32-bit elements; how exact they have to be, the bound alone decides.
No kernel may reach another device: no remote copies, remote signals or barrier semaphores. Data moves between devices by JAX's collectives and lax.ppermute only.
A program may use at most 128 MiB of HBM per device.

v0:
```python
import jax
import jax.numpy as jnp
from jax import lax
from jax.sharding import PartitionSpec as P

NV = 256
IRREPS = 8
VH = 32


def shards(amplitudes, residual_in, ladder_ints, occ_energy, virt_energy, virt_order):
    first_block, second_block, pair_count = amplitudes.shape
    rows = lax.dot_general(
        lax.all_gather(amplitudes, "ja", axis=1, tiled=True),
        ladder_ints,
        (((2,), (1,)), ((), ())),
        precision=lax.Precision.HIGHEST,
        preferred_element_type=jnp.float32,
    )
    swapped = lax.all_to_all(rows, "ia", split_axis=1, concat_axis=0, tiled=True)
    mirrored = jnp.swapaxes(swapped, 0, 1)
    direct = lax.all_to_all(rows, "ja", split_axis=1, concat_axis=2, tiled=True)
    partner = lax.all_to_all(mirrored, "ja", split_axis=1, concat_axis=2, tiled=True)
    partner = partner.reshape(first_block, second_block, IRREPS, VH, VH)
    partner = jnp.swapaxes(partner, 3, 4).reshape(first_block, second_block, pair_count)
    residual = residual_in + direct + partner
    onehot = (virt_order[:, None] == jnp.arange(NV, dtype=jnp.int32)[None, :]).astype(jnp.float32)
    grouped = jnp.dot(
        onehot, virt_energy, precision=lax.Precision.HIGHEST, preferred_element_type=jnp.float32
    ).reshape(IRREPS, VH)
    pair_energy = (grouped[:, :, None] + grouped[:, None, :]).reshape(pair_count)
    first_start = lax.axis_index("ia") * first_block
    second_start = lax.axis_index("ja") * second_block
    first_energy = lax.dynamic_slice_in_dim(occ_energy, first_start, first_block)
    second_energy = lax.dynamic_slice_in_dim(occ_energy, second_start, second_block)
    denominator = (
        pair_energy[None, None, :] - first_energy[:, None, None] - second_energy[None, :, None]
    )
    return (residual, amplitudes + residual / denominator)


def solution(mesh):
    placed = (P("ia", "ja", None), P("ia", "ja", None), P("ja", None), P(), P(), P())
    return jax.shard_map(
        shards,
        mesh=mesh,
        in_specs=placed,
        out_specs=(P("ia", "ja", None), P("ia", "ja", None)),
        check_vma=False,
    )
```

profile of v0, /device:TPU:1, one launch (start us, length us, event | category | flops | bytes accessed | tf_op | source)
XLA Modules:
  0.0 220.6 jit_solution(12038359198786186109)
XLA Ops:
  7.2 0.0 copy-start
  7.2 0.0 all-gather.2.cloned.1.call-start
  7.2 2.1 copy.31
  9.4 0.0 all-gather.2.cloned.1.call-update
  9.4 0.0 copy-start.3
  9.4 0.0 copy-start.2
  9.4 105.0 %all-gather.2.cloned.1.call-done = f32[8,64,8192]{2,0,1:T(8,128)} async-done(((f32[8,2,8192]{2,0,1:T(8,128)}), f32[8,64,8192]{2,0,1:T(8,128)}) %all-gather.2.cloned.1.call-update) | async-done | bytes 16777232 | tf_op jit(solution)/shard_map/all_gather | solution.py:14
  114.4 18.4 %fusion = f32[8,64,256]{2,0,1:T(8,128)} fusion(f32[8,64,8192]{2,0,1:T(8,128)} %all-gather.2.cloned.1.call-done, f32[256,8192]{1,0:T(8,128)} %param.8), kind=kOutput, calls=%fused_computation | convolution fusion | flops 12884901888 | bytes 25690112 | tf_op jit(solution)/shard_map/dot_general | solution.py:13
  132.8 0.0 copy-start.1
  132.8 23.8 %all_to_all.51 = f32[8,64,256]{2,0,1:T(8,128)S(1)} all-to-all(f32[8,64,256]{2,0,1:T(8,128)} %fusion), channel_id=1, replica_groups=mesh['ia'=8,'ja'=32] {'ia'}, dimensions={1} | all-to-all | bytes 1048576 | tf_op jit(solution)/shard_map/all_to_all | solution.py:20
  156.7 10.1 %all-to-all-start = ((f32[8,64,256]{2,0,1:T(8,128)}), f32[8,64,256]{2,0,1:T(8,128)S(1)}, u32[]{:S(2)}, u32[]{:S(2)}) async-start(f32[8,64,256]{2,0,1:T(8,128)} %fusion), calls=%async_computation | async-start | bytes 1048576 | tf_op jit(solution)/shard_map/all_to_all | solution.py:22
  166.8 0.0 copy-done.3
  166.8 0.1 dynamic_slice.7
  166.9 0.1 dynamic_slice.6
  167.0 0.0 copy-done
  167.0 0.0 copy-done.2
  167.0 0.2 fusion.3
  167.2 0.1 add.39
  167.3 0.2 broadcast_add_fusion
  167.5 0.1 add.43
  167.6 1.0 copy.35
  168.5 15.1 %all-to-all-done = f32[8,64,256]{2,0,1:T(8,128)S(1)} async-done(((f32[8,64,256]{2,0,1:T(8,128)}), f32[8,64,256]{2,0,1:T(8,128)S(1)}, u32[]{:S(2)}, u32[]{:S(2)}) %all-to-all-start) | async-done | bytes 524320 | tf_op jit(solution)/shard_map/all_to_all | solution.py:22
  183.6 3.7 %all-to-all-start.2 = ((f32[8,64,256]{2,0,1:T(8,128)}), f32[8,64,256]{2,0,1:T(8,128)S(1)}, u32[]{:S(2)}, u32[]{:S(2)}) async-start(f32[8,64,256]{2,0,1:T(8,128)} %bitcast.8), calls=%async_computation.2 | async-start | bytes 1048576 | tf_op jit(solution)/shard_map/all_to_all | solution.py:23
  187.3 0.1 broadcast_subtract_fusion
  187.4 0.8 copy.32
  188.2 16.0 %all-to-all-done.2 = f32[8,64,256]{2,0,1:T(8,128)S(1)} async-done(((f32[8,64,256]{2,0,1:T(8,128)}), f32[8,64,256]{2,0,1:T(8,128)S(1)}, u32[]{:S(2)}, u32[]{:S(2)}) %all-to-all-start.2) | async-done | bytes 524320 | tf_op jit(solution)/shard_map/all_to_all | solution.py:23
  204.2 0.3 copy.48
  204.5 0.5 reshape.58
  205.0 1.8 copy.37
  206.9 2.5 %reshape.59 = f32[8,2,8192]{2,0,1:T(8,128)S(1)} reshape(f32[8,2,8,32,32]{4,3,2,0,1:T(8,128)} %copy.37) | data formatting | bytes 1048576 | tf_op jit(solution)/shard_map/reshape | solution.py:25
  209.4 0.0 copy-done.1
  209.4 2.0 divide_add_fusion
  211.4 1.2 copy.40
  212.6 1.2 copy.39
Async XLA Ops:
  7.2 159.8 %copy-start = (f32[256]{0:T(256)S(1)}, f32[256]{0:T(256)}, u32[]{:S(2)}) copy-start(f32[256]{0:T(256)} %param.10) | copy-start | bytes 3076
  7.2 107.3 %all-gather.2.cloned.1.call-start = ((), (), s32[]{:S(2)}) async-start(), calls=%async_computation.3 | async-start | bytes 17301504 | tf_op jit(solution)/shard_map/all_gather | solution.py:14
  9.4 157.4 %copy-start.3 = (f32[64]{0:T(128)S(1)}, f32[64]{0:T(128)}, u32[]{:S(2)}) copy-start(f32[64]{0:T(128)} %param.9) | copy-start | bytes 772
  9.4 157.6 %copy-start.2 = (s32[256]{0:T(256)S(1)}, s32[256]{0:T(256)}, u32[]{:S(2)}) copy-start(s32[256]{0:T(256)} %param.11) | copy-start | bytes 3076
  132.8 76.6 %copy-start.1 = (f32[8,2,8192]{2,1,0:T(2,128)S(1)}, f32[8,2,8192]{2,1,0:T(2,128)}, u32[]{:S(2)}) copy-start(f32[8,2,8192]{2,1,0:T(2,128)} %param.6) | copy-start | bytes 1572868
  156.7 26.9 %all-to-all-start = ((f32[8,64,256]{2,0,1:T(8,128)}), f32[8,64,256]{2,0,1:T(8,128)S(1)}, u32[]{:S(2)}, u32[]{:S(2)}) async-start(f32[8,64,256]{2,0,1:T(8,128)} %fusion), calls=%async_computation | async-start | bytes 1048576 | tf_op jit(solution)/shard_map/all_to_all | solution.py:22
  183.6 20.6 %all-to-all-start.2 = ((f32[8,64,256]{2,0,1:T(8,128)}), f32[8,64,256]{2,0,1:T(8,128)S(1)}, u32[]{:S(2)}, u32[]{:S(2)}) async-start(f32[8,64,256]{2,0,1:T(8,128)} %bitcast.8), calls=%async_computation.2 | async-start | bytes 1048576 | tf_op jit(solution)/shard_map/all_to_all | solution.py:23
Sparse Core Ops, SparseCore 0:
  10.4 103.9 all-gather.1
where the time goes:
time: 221 us
  waiting for transfers between devices  136 us (62%)
  blocking collectives  23.8 us (11%)
  matrix products  18.6 us (8%)
  between operations  14.1 us (6%)
  starting transfers between devices  13.9 us (6%)
  local copies, waits for them, and re-layouts  11.8 us (5%)
  other arithmetic  2.24 us (1%)
    all_gather x1, waiting for transfers between devices, shards(): lax.all_gather(amplitudes, 'ja', axis=1, tiled=True)  105 us
    all_to_all x1, blocking collectives, shards(): lax.all_to_all(rows, 'ia', split_axis=1, concat_axis=0, tiled=True)  23.8 us
    dot_general x1, matrix products, shards(): lax.dot_general(lax.all_gather(amplitudes, 'ja', axis=1, tiled=True), lad...  18.4 us
    all_to_all x1, waiting for transfers between devices, shards(): lax.all_to_all(mirrored, 'ja', split_axis=1, concat_axis=2, tiled=True)  16 us
    all_to_all x1, waiting for transfers between devices, shards(): direct = lax.all_to_all(rows, 'ja', split_axis=1, concat_axis=2, tiled=True)  15.1 us
    all_to_all x1, starting transfers between devices, shards(): direct = lax.all_to_all(rows, 'ja', split_axis=1, concat_axis=2, tiled=True)  10.1 us
    unnamed x11, local copies, waits for them, and re-layouts  4.57 us
  transfers between devices with their start and end apart: 3, of which 3 were waited for; matrix products, arithmetic and copies ran while one was open for 1% of the time, Pallas kernels for 0%

commit v1 on v0

--- a/solution.py
+++ b/solution.py
@@ -14,13 +14,14 @@
         lax.all_gather(amplitudes, "ja", axis=1, tiled=True),
         ladder_ints,
         (((2,), (1,)), ((), ())),
-        precision=lax.Precision.HIGHEST,
+        precision=lax.Precision.HIGH,
         preferred_element_type=jnp.float32,
     )
     swapped = lax.all_to_all(rows, "ia", split_axis=1, concat_axis=0, tiled=True)
     mirrored = jnp.swapaxes(swapped, 0, 1)
-    direct = lax.all_to_all(rows, "ja", split_axis=1, concat_axis=2, tiled=True)
-    partner = lax.all_to_all(mirrored, "ja", split_axis=1, concat_axis=2, tiled=True)
+    both = jnp.stack([rows, mirrored])
+    both = lax.all_to_all(both, "ja", split_axis=2, concat_axis=3, tiled=True)
+    direct, partner = both[0], both[1]
     partner = partner.reshape(first_block, second_block, IRREPS, VH, VH)
     partner = jnp.swapaxes(partner, 3, 4).reshape(first_block, second_block, pair_count)
     residual = residual_in + direct + partner

time: 221 us -> 210 us (0.950)
  blocking collectives: 23.8 us -> 0 us
  waiting for transfers between devices: 136 us -> 145 us
  starting transfers between devices: 13.9 us -> 19.3 us
  matrix products: 18.6 us -> 14.1 us
  local copies, waits for them, and re-layouts: 11.8 us -> 14.5 us
    all_to_all x1 -> x0, blocking collectives: 23.8 us -> none  [shards(): lax.all_to_all(rows, 'ia', split_axis=1, concat_axis=0, tiled=True)]
    all_to_all x2, waiting for transfers between devices: 31.1 us -> 40 us  [the longest x1 27 us: shards(): both = lax.all_to_all(both, 'ja', split_axis=2, concat_axis=3, tiled=True)]
    all_to_all x2, starting transfers between devices: 13.8 us -> 19.2 us  [the longest x1 10.1 us: shards(): both = lax.all_to_all(both, 'ja', split_axis=2, concat_axis=3, tiled=True)]
    dot_general x1, matrix products: 18.4 us -> 13.9 us  [shards(): lax.dot_general(lax.all_gather(amplitudes, 'ja', axis=1, tiled=True), lad...]
where the time goes in v1:
time: 210 us; the launch traced here: 209 us
  waiting for transfers between devices  145 us (69%)
  starting transfers between devices  19.3 us (9%)
  local copies, waits for them, and re-layouts  14.5 us (7%)
  matrix products  14.1 us (7%)
  between operations  14.1 us (7%)
  other arithmetic  2.26 us (1%)
    all_gather x1, waiting for transfers between devices, shards(): lax.all_gather(amplitudes, 'ja', axis=1, tiled=True)  105 us
    all_to_all x1, waiting for transfers between devices, shards(): both = lax.all_to_all(both, 'ja', split_axis=2, concat_axis=3, tiled=True)  27 us
    dot_general x1, matrix products, shards(): lax.dot_general(lax.all_gather(amplitudes, 'ja', axis=1, tiled=True), lad...  13.9 us
    all_to_all x1, waiting for transfers between devices, shards(): lax.all_to_all(rows, 'ia', split_axis=1, concat_axis=0, tiled=True)  13 us
    all_to_all x1, starting transfers between devices, shards(): both = lax.all_to_all(both, 'ja', split_axis=2, concat_axis=3, tiled=True)  10.1 us
    all_to_all x1, starting transfers between devices, shards(): lax.all_to_all(rows, 'ia', split_axis=1, concat_axis=0, tiled=True)  9.12 us
    unnamed x11, local copies, waits for them, and re-layouts  4.56 us
  transfers between devices with their start and end apart: 3, of which 3 were waited for; matrix products, arithmetic and copies ran while one was open for 1% of the time, Pallas kernels for 0%

profile of v1, /device:TPU:1, one launch (start us, length us, event | category | flops | bytes accessed | tf_op | source)
XLA Modules:
  0.0 209.3 jit_solution(7992488035059534277)
XLA Ops:
  7.2 0.0 copy-start
  7.2 0.0 all-gather.2.cloned.1.call-start
  7.2 2.1 %copy.20 = f32[8,2,8192]{2,0,1:T(8,128)} copy(f32[8,2,8192]{2,1,0:T(2,128)} %param.6) | data formatting | bytes 1048576 | tf_op args[0]
  9.4 0.0 all-gather.2.cloned.1.call-update
  9.4 105.1 %all-gather.2.cloned.1.call-done = f32[8,64,8192]{2,0,1:T(8,128)} async-done(((f32[8,2,8192]{2,0,1:T(8,128)}), f32[8,64,8192]{2,0,1:T(8,128)}) %all-gather.2.cloned.1.call-update) | async-done | bytes 16777232 | tf_op jit(solution)/shard_map/all_gather | solution.py:14
  114.4 13.9 %fusion = f32[8,64,256]{2,0,1:T(8,128)} fusion(f32[8,64,8192]{2,0,1:T(8,128)} %all-gather.2.cloned.1.call-done, f32[256,8192]{1,0:T(8,128)} %param.8), kind=kOutput, calls=%fused_computation | convolution fusion | flops 6442450944 | bytes 25690112 | tf_op jit(solution)/shard_map/dot_general | solution.py:13
  128.3 0.0 copy-start.2
  128.3 0.0 copy-start.3
  128.3 9.1 %all-to-all-start = ((f32[8,64,256]{2,0,1:T(8,128)}), f32[8,64,256]{2,0,1:T(8,128)S(1)}, u32[]{:S(2)}, u32[]{:S(2)}) async-start(f32[8,64,256]{2,0,1:T(8,128)} %fusion), calls=%async_computation | async-start | bytes 1048576 | tf_op jit(solution)/shard_map/all_to_all | solution.py:20
  137.4 1.2 copy.43
  138.7 13.0 %all-to-all-done = f32[8,64,256]{2,0,1:T(8,128)S(1)} async-done(((f32[8,64,256]{2,0,1:T(8,128)}), f32[8,64,256]{2,0,1:T(8,128)S(1)}, u32[]{:S(2)}, u32[]{:S(2)}) %all-to-all-start) | async-done | bytes 524320 | tf_op jit(solution)/shard_map/all_to_all | solution.py:20
  151.7 0.1 pad_maximum_fusion
  151.8 1.6 copy.24
  153.4 0.0 copy-start.1
  153.4 10.1 %all-to-all-start.1 = ((f32[2,8,64,256]{3,1,0,2:T(8,128)}), f32[2,8,64,256]{3,1,0,2:T(8,128)S(1)}, u32[]{:S(2)}, u32[]{:S(2)}) async-start(f32[2,8,64,256]{3,1,0,2:T(8,128)} %copy.24), calls=%async_computation.1 | async-start | bytes 2097152 | tf_op jit(solution)/shard_map/all_to_all | solution.py:23
  163.5 0.0 copy-done
  163.5 0.0 copy-done.2
  163.5 0.2 fusion.3
  163.8 0.0 copy-done.3
  163.8 0.1 dynamic_slice.7
  163.9 0.1 dynamic_slice.6
  164.0 0.1 add.39
  164.1 0.1 broadcast_add_fusion
  164.2 0.1 add.43
  164.3 0.1 broadcast_subtract_fusion
  164.4 27.0 %all-to-all-done.1 = f32[2,8,64,256]{3,1,0,2:T(8,128)S(1)} async-done(((f32[2,8,64,256]{3,1,0,2:T(8,128)}), f32[2,8,64,256]{3,1,0,2:T(8,128)S(1)}, u32[]{:S(2)}, u32[]{:S(2)}) %all-to-all-start.1) | async-done | bytes 1048608 | tf_op jit(solution)/shard_map/all_to_all | solution.py:23
  191.4 0.6 copy.42
  192.0 0.1 fusion.6
  192.1 1.1 copy.26
  193.2 0.5 reshape_squeeze.3
  193.7 1.8 copy.28
  195.5 2.5 %reshape.58 = f32[8,2,8192]{2,0,1:T(8,128)S(1)} reshape(f32[8,2,8,32,32]{4,3,2,0,1:T(8,128)} %copy.28) | data formatting | bytes 1048576 | tf_op jit(solution)/shard_map/reshape | solution.py:26
  198.1 0.0 copy-done.1
  198.1 2.0 divide_add_fusion
  200.0 1.2 copy.31
  201.2 1.2 copy.30
  (1 shorter events, 0.0 us)
Async XLA Ops:
  7.2 156.3 %copy-start = (f32[256]{0:T(256)S(1)}, f32[256]{0:T(256)}, u32[]{:S(2)}) copy-start(f32[256]{0:T(256)} %param.10) | copy-start | bytes 3076
  7.2 107.3 %all-gather.2.cloned.1.call-start = ((), (), s32[]{:S(2)}) async-start(), calls=%async_computation.2 | async-start | bytes 17301504 | tf_op jit(solution)/shard_map/all_gather | solution.py:14
  128.3 35.2 %copy-start.2 = (s32[256]{0:T(256)S(1)}, s32[256]{0:T(256)}, u32[]{:S(2)}) copy-start(s32[256]{0:T(256)} %param.11) | copy-start | bytes 3076
  128.3 35.5 %copy-start.3 = (f32[64]{0:T(128)S(1)}, f32[64]{0:T(128)}, u32[]{:S(2)}) copy-start(f32[64]{0:T(128)} %param.9) | copy-start | bytes 772
  128.3 23.4 %all-to-all-start = ((f32[8,64,256]{2,0,1:T(8,128)}), f32[8,64,256]{2,0,1:T(8,128)S(1)}, u32[]{:S(2)}, u32[]{:S(2)}) async-start(f32[8,64,256]{2,0,1:T(8,128)} %fusion), calls=%async_computation | async-start | bytes 1048576 | tf_op jit(solution)/shard_map/all_to_all | solution.py:20
  153.4 44.7 %copy-start.1 = (f32[8,2,8192]{2,1,0:T(2,128)S(1)}, f32[8,2,8192]{2,1,0:T(2,128)}, u32[]{:S(2)}) copy-start(f32[8,2,8192]{2,1,0:T(2,128)} %param.6) | copy-start | bytes 1572868
  153.4 38.0 %all-to-all-start.1 = ((f32[2,8,64,256]{3,1,0,2:T(8,128)}), f32[2,8,64,256]{3,1,0,2:T(8,128)S(1)}, u32[]{:S(2)}, u32[]{:S(2)}) async-start(f32[2,8,64,256]{3,1,0,2:T(8,128)} %copy.24), calls=%async_computation.1 | async-start | bytes 2097152 | tf_op jit(solution)/shard_map/all_to_all | solution.py:23
Sparse Core Ops, SparseCore 0:
  10.4 103.9 all-gather.1

commit v2 on v0

v2 whole, which is shorter than its diff:
```python
import jax
import jax.numpy as jnp
import numpy as np
from jax import lax
from jax.experimental import pallas as pl
from jax.experimental.pallas import tpu as pltpu
from jax.sharding import PartitionSpec as P

NV = 256
IRREPS = 8
VH = 32
NP = 8192
HALF = NP // 2
TILE = 512
ROWS = 256
COLS = 256
BOTH = ("ia", "ja")
F32 = jnp.float32
BF16 = jnp.bfloat16
VMEM_LIMIT = 40 * 1024 * 1024


def device_at(x, y, z, c):
    z = z % 8
    return (z // 4 * 4 + x % 4) * 32 + (y % 4) * 8 + (z % 4) * 2 + c % 2


def moved(dy=0, dz=0, dc=0):
    return [
        (device_at(x, y, z, c), device_at(x, y + dy, z + dz, c + dc))
        for x in range(4)
        for y in range(4)
        for z in range(8)
        for c in range(2)
    ]


def shift(array, dy=0, dz=0, dc=0):
    return lax.ppermute(array, BOTH, moved(dy, dz, dc))


X_GROUPS = [
    [device_at(x, y, z, c) for x in range(4) for c in range(2)] for y in range(4) for z in range(8)
]


def split(value):
    high = value.astype(BF16)
    return high, (value - high.astype(F32)).astype(BF16)


def accumulate(pieces, own, partner, total, step):
    t_high, t_low = split(jnp.concatenate([piece[...] for piece in pieces], axis=0))
    v_high, v_low = split(jnp.concatenate([own[...], partner[...]], axis=0))
    dims = (((1,), (1,)), ((), ()))
    part = lax.dot_general(t_high, v_low, dims, preferred_element_type=F32)
    part += lax.dot_general(t_low, v_high, dims, preferred_element_type=F32)
    part += lax.dot_general(t_high, v_high, dims, preferred_element_type=F32)

    @pl.when(step == 0)
    def _():
        total[...] = part

    @pl.when(step != 0)
    def _():
        total[...] += part


def slot_of(dy, side, dz):
    return dy * 8 + side * 4 + dz


def first_half_kernel(slots, *refs):
    count = len(refs) - 4
    own, partner, out, total = refs[count:]
    step = pl.program_id(0)
    accumulate(refs[:count], own, partner, total, step)

    @pl.when(step == pl.num_programs(0) - 1)
    def _():
        for block, slot in enumerate(slots):
            for v in range(2):
                out[v, slot] = total[block * 8 : block * 8 + 8, v * COLS : (v + 1) * COLS]


def second_half_kernel(slots, place, *refs):
    count = len(refs) - 14
    own, partner, first = refs[count : count + 3]
    direct, crossed = refs[count + 3 : count + 11], refs[count + 11]
    total, sums = refs[count + 12 :]
    step = pl.program_id(0)
    accumulate(refs[:count], own, partner, total, step)

    @pl.when(step == pl.num_programs(0) - 1)
    def _():
        for block, slot in enumerate(slots):
            dy, side, dz = slot // 8, slot // 4 % 2, slot % 4
            for v in range(2):
                value = first[v, slot] + total[block * 8 : block * 8 + 8, v * COLS : (v + 1) * COLS]
                sums[v, slot] = value
                direct[side * 4 + dz][dy, v] = value
        y, z, c = place[1], place[2], place[3]
        for to in range(4):
            for k in range(2):
                for m in range(2):
                    z_low = to % 2 * 2 + m
                    dy = lax.rem(2 * k + to // 2 - y + 4, 4)
                    up = dy * 8 + lax.rem(z - z_low + 4, 4)
                    down = dy * 8 + 4 + lax.rem(z_low - z + 8, 4)
                    for core in range(2):
                        v = lax.rem(c + core, 2)
                        a, b = sums[v, up], sums[v, down]
                        crossed[2 * to, k, m, core] = jnp.concatenate([a[:4], b[:4]], axis=0)
                        crossed[2 * to + 1, k, m, core] = jnp.concatenate([a[4:], b[4:]], axis=0)


def z_pack_kernel(place, came, *outs):
    z = place[2]
    for d in range(8):
        to = lax.rem(z + d, 8)
        k, x_low, side = to // 4, lax.rem(to // 2, 2), lax.rem(to, 2)
        for x_high in range(2):
            for source in range(2):
                at = (2 * x_high + x_low) * 2 + source
                for core in range(2):
                    parts = []
                    for m in range(2):
                        block = came[at, k, m, core]
                        parts.append(jnp.where(side == 0, block[:4], block[4:]))
                    outs[d][x_high, source, core] = jnp.concatenate(parts, axis=0)


def y_pack_kernel(place, *refs):
    came, outs, held = refs[:8], refs[8:12], refs[12]
    for d in range(8):
        held[d] = came[d][...]
    x, y, z = place[0], place[1], place[2]
    side = lax.rem(z, 2)
    for e in range(4):
        to = lax.rem(y + e, 4)
        z_high, x_high = to // 2, lax.rem(to, 2)
        for z_low in range(4):
            froms = []
            for m in range(2):
                low = lax.rem(x, 2) * 2 + m
                up = lax.rem(z_high * 4 + low + lax.rem(z_low - low + 4, 4), 8)
                down = lax.rem(z_high * 4 + low - lax.rem(low - z_low + 4, 4) + 8, 8)
                froms.append(lax.rem(z - jnp.where(side == 0, up, down) + 8, 8))
            for source in range(2):
                for core in range(2):
                    a = held[froms[0], x_high, source, core]
                    b = held[froms[1], x_high, source, core]
                    outs[e][z_low, source, core] = jnp.concatenate([a[:4], b[4:]], axis=0)


def direct_pack_kernel(*refs):
    came, outs = refs[:8], refs[8:]
    for dy in range(4):
        for n in range(8):
            outs[dy][n] = came[n][dy]


def final_kernel(place, *refs):
    direct, mirror = refs[:4], refs[4:8]
    t_ref, r_ref, pair, first, second, turn, residual, updated, moved_ref = refs[8:]
    y, z, c = place[1], place[2], place[3]
    order = (0, 2, 1, 3)
    for e in range(4):
        for z_low in range(4):
            for core in range(2):
                a, b = mirror[e][z_low, 0, core], mirror[e][z_low, 1, core]
                rows = [s[m * 4 + n : m * 4 + n + 1] for m in range(2) for s in (a, b) for n in order]
                column = (z_low % 2 * 2 + core) * COLS
                group = e * 2 + z_low // 2
                moved_ref[group * 16 : group * 16 + 16, column : column + COLS] = jnp.concatenate(rows, axis=0)
    value = moved_ref[...]
    high = value.astype(BF16)
    rest = value - high.astype(F32)
    middle = rest.astype(BF16)
    low = (rest - middle.astype(F32)).astype(BF16)
    dims = (((1,), (0,)), ((), ()))
    turned = lax.dot_general(high, turn[...], dims, preferred_element_type=F32)
    turned += lax.dot_general(middle, turn[...], dims, preferred_element_type=F32)
    turned += lax.dot_general(low, turn[...], dims, preferred_element_type=F32)
    moved_ref[...] = turned
    for e in range(4):
        source = lax.rem(y - e + 4, 4)
        for z_low in range(4):
            up = lax.rem(z_low - z + 8, 4)
            down = 4 + lax.rem(z - z_low + 4, 4)
            for core in range(2):
                v = lax.rem(c + core, 2)
                column = (z_low % 2 * 2 + core) * COLS
                group = e * 2 + z_low // 2
                at = pl.ds(pl.multiple_of(source * 2048 + z_low * 512 + core * COLS, COLS), COLS)
                straight = jnp.concatenate([direct[e][up, v], direct[e][down, v]], axis=0)
                total = r_ref[:, at] + straight + moved_ref[group * 16 : group * 16 + 16, column : column + COLS]
                residual[:, at] = total
                updated[:, at] = t_ref[:, at] + total / (pair[:, at] - first[...] - second[...])


SMEM = pl.BlockSpec(memory_space=pltpu.SMEM)
VMEM = pl.BlockSpec(memory_space=pltpu.VMEM)
PARAMS = pltpu.CompilerParams(vmem_limit_bytes=VMEM_LIMIT)


def shape(*dims):
    return jax.ShapeDtypeStruct(dims, F32)


def tiles(rows, offset):
    return pl.BlockSpec((rows, TILE), lambda k: (0, k + offset))


def shards(amplitudes, residual_in, ladder_ints, occ_energy, virt_energy, virt_order):
    ia, ja = lax.axis_index("ia"), lax.axis_index("ja")
    place = jnp.stack([ia % 4, ja // 8, ia // 4 * 4 + ja // 2 % 4, ja % 2]).astype(jnp.int32)
    own = amplitudes.reshape(16, NP)

    from_below, from_above = shift(own, dy=1), shift(own, dy=-1)
    up, down = [shift(own[:8], dz=1)], [shift(own[8:], dz=-1)]
    up.append(shift(up[-1], dz=1))
    down.append(shift(down[-1], dz=-1))
    far_up, far_down = shift(from_below[:8], dy=1), shift(from_above[8:], dy=-1)
    up.append(shift(up[-1], dz=1))
    down.append(shift(down[-1], dz=-1))
    partner = shift(ladder_ints, dc=1)

    low = [array[:, :HALF] for array in up + down]
    low = jnp.concatenate(low, axis=0)
    low_below, low_above = shift(low, dy=1), shift(low, dy=-1)
    low_far_up, low_far_down = shift(low_below[:24], dy=1), shift(low_above[24:], dy=-1)

    high_up = jnp.concatenate([from_below[:8, HALF:], from_above[:8, HALF:], far_up[:, HALF:]], axis=0)
    high_down = jnp.concatenate([from_below[8:, HALF:], from_above[8:, HALF:], far_down[:, HALF:]], axis=0)
    high_ups, high_downs = [], []
    for _ in range(3):
        high_up, high_down = shift(high_up, dz=1), shift(high_down, dz=-1)
        high_ups.append(high_up)
        high_downs.append(high_down)

    near = [own, from_below, from_above, far_up, far_down] + up + down
    near_slots = [slot_of(dy, side, 0) for dy in (0, 3, 1) for side in range(2)]
    near_slots += [slot_of(2, 0, 0), slot_of(2, 1, 0)]
    near_slots += [slot_of(0, side, dz) for side in range(2) for dz in (1, 2, 3)]
    low_pieces = [low_below, low_above, low_far_up, low_far_down]
    low_slots = [slot_of(dy, side, dz) for dy in (3, 1) for side in range(2) for dz in (1, 2, 3)]
    low_slots += [slot_of(2, side, dz) for side in range(2) for dz in (1, 2, 3)]
    high_pieces = high_ups + high_downs
    high_slots = [slot_of(dy, side, dz) for side in range(2) for dz in (1, 2, 3) for dy in (3, 1, 2)]

    steps = HALF // TILE
    cost = pl.CostEstimate(flops=2 * 3 * ROWS * 2 * COLS * HALF, bytes_accessed=12 << 20, transcendentals=0)
    whole = pl.BlockSpec((2, 32, 8, COLS), lambda k: (0, 0, 0, 0))
    first = pl.pallas_call(
        lambda *refs: first_half_kernel(near_slots + low_slots, *refs),
        grid=(steps,),
        in_specs=[tiles(p.shape[0], 0) for p in near + low_pieces] + [tiles(COLS, 0)] * 2,
        out_specs=whole,
        out_shape=shape(2, 32, 8, COLS),
        scratch_shapes=[pltpu.VMEM((ROWS, 2 * COLS), F32)],
        compiler_params=PARAMS,
        cost_estimate=cost,
        name="first_half",
    )(*near, *low_pieces, ladder_ints, partner)
    sent = pl.BlockSpec((4, 2, 8, COLS), lambda k: (0, 0, 0, 0))
    *direct, crossed = pl.pallas_call(
        lambda place, *refs: second_half_kernel(near_slots + high_slots, place, *refs),
        grid=(steps,),
        in_specs=[SMEM]
        + [tiles(p.shape[0], steps) for p in near]
        + [tiles(p.shape[0], 0) for p in high_pieces]
        + [tiles(COLS, steps)] * 2
        + [whole],
        out_specs=[sent] * 8 + [pl.BlockSpec((8, 2, 2, 2, 8, COLS), lambda k: (0, 0, 0, 0, 0, 0))],
        out_shape=[shape(4, 2, 8, COLS)] * 8 + [shape(8, 2, 2, 2, 8, COLS)],
        scratch_shapes=[pltpu.VMEM((ROWS, 2 * COLS), F32), pltpu.VMEM((2, 32, 8, COLS), F32)],
        compiler_params=PARAMS,
        cost_estimate=cost,
        name="second_half",
    )(place, *near, *high_pieces, ladder_ints, partner, first)

    came = lax.all_to_all(crossed, BOTH, 0, 0, axis_index_groups=X_GROUPS)
    for n in range(8):
        dz = n % 4
        if dz:
            direct[n] = shift(direct[n], dz=-dz if n < 4 else dz)
    z_sent = pl.pallas_call(
        z_pack_kernel,
        in_specs=[SMEM, VMEM],
        out_specs=[VMEM] * 8,
        out_shape=[shape(2, 2, 2, 8, COLS)] * 8,
        compiler_params=PARAMS,
        name="z_pack",
    )(place, came)
    z_came = [z_sent[0]] + [shift(z_sent[d], dz=d) for d in range(1, 8)]
    direct = pl.pallas_call(
        direct_pack_kernel,
        in_specs=[VMEM] * 8,
        out_specs=[VMEM] * 4,
        out_shape=[shape(8, 2, 8, COLS)] * 4,
        compiler_params=PARAMS,
        name="direct_pack",
    )(*direct)
    direct = [direct[0]] + [shift(direct[dy], dy=dy) for dy in range(1, 4)]
    y_sent = pl.pallas_call(
        y_pack_kernel,
        in_specs=[SMEM] + [VMEM] * 8,
        out_specs=[VMEM] * 4,
        out_shape=[shape(4, 2, 2, 8, COLS)] * 4,
        scratch_shapes=[pltpu.VMEM((8, 2, 2, 2, 8, COLS), F32)],
        compiler_params=PARAMS,
        name="y_pack",
    )(place, *z_came)
    mirror = [y_sent[0]] + [shift(y_sent[e], dy=e) for e in range(1, 4)]

    onehot = (virt_order[:, None] == jnp.arange(NV, dtype=jnp.int32)[None, :]).astype(F32)
    grouped = jnp.dot(
        onehot, virt_energy, precision=lax.Precision.HIGHEST, preferred_element_type=F32
    ).reshape(IRREPS, VH)
    pair_energy = (grouped[:, :, None] + grouped[:, None, :]).reshape(1, NP)
    first_energy = jnp.repeat(lax.dynamic_slice_in_dim(occ_energy, ia * 8, 8), 2).reshape(16, 1)
    second_energy = jnp.tile(lax.dynamic_slice_in_dim(occ_energy, ja * 2, 2), 8).reshape(16, 1)
    spot = jnp.arange(VH * VH, dtype=jnp.int32)
    turn = (spot[None, :] == (spot % VH * VH + spot // VH)[:, None]).astype(BF16)
    residual, updated = pl.pallas_call(
        final_kernel,
        in_specs=[SMEM] + [VMEM] * 14,
        out_specs=[VMEM] * 2,
        out_shape=[shape(16, NP)] * 2,
        scratch_shapes=[pltpu.VMEM((128, VH * VH), F32)],
        compiler_params=PARAMS,
        name="final",
    )(
        place, *direct, *mirror, own, residual_in.reshape(16, NP), pair_energy, first_energy, second_energy, turn
    )
    return residual.reshape(8, 2, NP), updated.reshape(8, 2, NP)


def solution(mesh):
    placed = (P("ia", "ja", None), P("ia", "ja", None), P("ja", None), P(), P(), P())
    return jax.shard_map(
        shards,
        mesh=mesh,
        in_specs=placed,
        out_specs=(P("ia", "ja", None), P("ia", "ja", None)),
        check_vma=False,
    )
```

time: 221 us -> 158 us (0.71)
  waiting for transfers between devices: 136 us -> 22.4 us
  starting transfers between devices: 13.9 us -> 79.9 us
  Pallas kernels: 0 us -> 25.3 us
  blocking collectives: 23.8 us -> 0 us
  matrix products: 18.6 us -> 0.25 us
  local copies, waits for them, and re-layouts: 11.8 us -> 26.1 us
  between operations: 14.1 us -> 0.95 us
    all_gather x1 -> x0, waiting for transfers between devices: 105 us -> none  [shards(): lax.all_gather(amplitudes, 'ja', axis=1, tiled=True)]
    ppermute x0 -> x40, starting transfers between devices: none -> 68.8 us  [shift(): return lax.ppermute(array, BOTH, moved(dy, dz, dc))]
    all_to_all x2 -> x1, waiting for transfers between devices: 31.1 us -> 2.11 us  [shards(): came = lax.all_to_all(crossed, BOTH, 0, 0, axis_index_groups=X_GROUPS)]
    pallas_call x0 -> x6, Pallas kernels: none -> 25.3 us  [the longest x1 9.99 us: shards(): pl.pallas_call(lambda place, *refs: second_half_kernel(near_slots + high_...]
    all_to_all x1 -> x0, blocking collectives: 23.8 us -> none  [shards(): lax.all_to_all(rows, 'ia', split_axis=1, concat_axis=0, tiled=True)]
    ppermute x0 -> x40, waiting for transfers between devices: none -> 20.3 us  [shift(): return lax.ppermute(array, BOTH, moved(dy, dz, dc))]
    dot_general x1 -> x0, matrix products: 18.4 us -> none  [shards(): lax.dot_general(lax.all_gather(amplitudes, 'ja', axis=1, tiled=True), lad...]
    unnamed x11 -> x63, local copies, waits for them, and re-layouts: 4.57 us -> 14.4 us
  transfers between devices with their start and end apart: 3 -> 41, of which waited for: 3 -> 12; matrix products, arithmetic and copies ran while one was open for 1% -> 5% of each run, Pallas kernels for 0% -> 8%
where the time goes in v2:
time: 158 us; the launch traced here: 156 us
  starting transfers between devices  79.9 us (51%)
  local copies, waits for them, and re-layouts  26.1 us (17%)
  Pallas kernels  25.3 us (16%)
  waiting for transfers between devices  22.4 us (14%)
    ppermute x40, starting transfers between devices, shift(): return lax.ppermute(array, BOTH, moved(dy, dz, dc))  68.8 us
    ppermute x40, waiting for transfers between devices, shift(): return lax.ppermute(array, BOTH, moved(dy, dz, dc))  20.3 us
    unnamed x63, local copies, waits for them, and re-layouts  14.4 us
    all_to_all x1, starting transfers between devices, shards(): came = lax.all_to_all(crossed, BOTH, 0, 0, axis_index_groups=X_GROUPS)  11 us
    pallas_call x1, Pallas kernels, shards(): pl.pallas_call(lambda place, *refs: second_half_kernel(near_slots + high_...  9.99 us
    pallas_call x1, Pallas kernels, shards(): pl.pallas_call(lambda *refs: first_half_kernel(near_slots + low_slots, *r...  8.87 us
    reshape x2, local copies, waits for them, and re-layouts, shards(): return (residual.reshape(8, 2, NP), updated.reshape(8, 2, NP))  4.27 us
  transfers between devices with their start and end apart: 41, of which 12 were waited for; matrix products, arithmetic and copies ran while one was open for 5% of the time, Pallas kernels for 8%

profile of v2, /device:TPU:1, one launch (start us, length us, event | category | flops | bytes accessed | tf_op | source)
XLA Modules:
  0.0 156.1 jit_solution(511824629246890313)
XLA Ops:
  0.6 1.1 fusion.14
  1.9 2.5 %collective-permute-start.4 = (f32[8,8192]{1,0:T(8,128)S(1)}, f32[8,8192]{1,0:T(8,128)S(1)}, u32[]{:S(2)}, u32[]{:S(2)}) collective-permute-start(f32[8,8192]{1,0:T(8,128)S(1)} %slice.63), channel_id=1, source_target_pairs={{0,2},{1,3},{2,4},{3,5},{4,6},{5,7},{6,128},{7,129},{128,130},{129... | collective-permute-start | bytes 786440 | tf_op jit(solution)/shard_map/ppermute | solution.py:39
  4.5 1.4 reshape.67.refs_0_.refs_8_
  5.9 1.4 collective-permute-start
  7.2 1.5 collective-permute-start.1
  8.9 4.0 %collective-permute-start.7 = (f32[8,8192]{1,0:T(8,128)S(1)}, f32[8,8192]{1,0:T(8,128)S(1)}, u32[]{:S(2)}, u32[]{:S(2)}) collective-permute-start(f32[8,8192]{1,0:T(8,128)S(1)} %slice.65), channel_id=1, source_target_pairs={{0,134},{1,135},{2,0},{3,1},{4,2},{5,3},{6,4},{7,5},{128,6},{129,7... | collective-permute-start | bytes 786440 | tf_op jit(solution)/shard_map/ppermute | solution.py:39
  13.0 1.4 collective-permute-start.16
  14.4 3.0 %collective-permute-done.7.refs_8_ = f32[8,8192]{1,0:T(8,128)S(1)} collective-permute-done((f32[8,8192]{1,0:T(8,128)S(1)}, f32[8,8192]{1,0:T(8,128)S(1)}, u32[]{:S(2)}, u32[]{:S(2)}) %collective-permute-start.7) | collective-permute-done | bytes 262176 | tf_op jit(solution)/shard_map/ppermute | solution.py:39
  17.5 3.4 %collective-permute-start.8 = (f32[8,8192]{1,0:T(8,128)S(1)}, f32[8,8192]{1,0:T(8,128)S(1)}, u32[]{:S(2)}, u32[]{:S(2)}) collective-permute-start(f32[8,8192]{1,0:T(8,128)S(1)} %collective-permute-done.7.refs_8_), channel_id=1, source_target_pairs={{0,134},{1,135},{2,0},{3,1},{4,2},{5,3},{6,4},{7,5},{128,6},{129,7... | collective-permute-start | bytes 786440 | tf_op jit(solution)/shard_map/ppermute | solution.py:39
  21.0 2.7 %collective-permute-start.3 = (f32[8,8192]{1,0:T(8,128)S(1)}, f32[8,8192]{1,0:T(8,128)S(1)}, u32[]{:S(2)}, u32[]{:S(2)}) collective-permute-start(f32[8,8192]{1,0:T(8,128)S(1)} %slice.81), channel_id=1, source_target_pairs={{0,24},{1,25},{2,26},{3,27},{4,28},{5,29},{6,30},{7,31},{128,152},... | collective-permute-start | bytes 786440 | tf_op jit(solution)/shard_map/ppermute | solution.py:39
  24.5 3.4 %collective-permute-start.9 = (f32[8,8192]{1,0:T(8,128)S(1)}, f32[8,8192]{1,0:T(8,128)S(1)}, u32[]{:S(2)}, u32[]{:S(2)}) collective-permute-start(f32[8,8192]{1,0:T(8,128)S(1)} %collective-permute-done.8.refs_9_), channel_id=1, source_target_pairs={{0,134},{1,135},{2,0},{3,1},{4,2},{5,3},{6,4},{7,5},{128,6},{129,7... | collective-permute-start | bytes 786440 | tf_op jit(solution)/shard_map/ppermute | solution.py:39
  27.9 2.8 %collective-permute-done.6.refs_7_ = f32[8,8192]{1,0:T(8,128)S(1)} collective-permute-done((f32[8,8192]{1,0:T(8,128)S(1)}, f32[8,8192]{1,0:T(8,128)S(1)}, u32[]{:S(2)}, u32[]{:S(2)}) %collective-permute-start.6) | collective-permute-done | bytes 262176 | tf_op jit(solution)/shard_map/ppermute | solution.py:39
  31.9 2.7 %collective-permute-start.18 = (f32[48,4096]{1,0:T(8,128)S(1)}, f32[48,4096]{1,0:T(8,128)S(1)}, u32[]{:S(2)}, u32[]{:S(2)}) collective-permute-start(f32[48,4096]{1,0:T(8,128)S(1)} %slice_dynamic-update-slice_fusion), channel_id=1, source_target_pairs={{0,24},{1,25},{2,26},{3,27},{4,28},{5,29},{6,30},{7,31},{128,152},... | collective-permute-start | bytes 2359304 | tf_op jit(solution)/shard_map/ppermute | solution.py:39
  34.7 1.6 collective-permute-start.10
  36.3 1.9 %collective-permute-start.13 = (f32[24,4096]{1,0:T(8,128)S(1)}, f32[24,4096]{1,0:T(8,128)}, u32[]{:S(2)}, u32[]{:S(2)}) collective-permute-start(f32[24,4096]{1,0:T(8,128)S(1)} %pad_maximum_fusion.1), channel_id=1, source_target_pairs={{0,134},{1,135},{2,0},{3,1},{4,2},{5,3},{6,4},{7,5},{128,6},{129,7... | collective-permute-start | bytes 1179656 | tf_op jit(solution)/shard_map/ppermute | solution.py:39
  38.2 5.1 %collective-permute-done.10.refs_11_ = f32[24,4096]{1,0:T(8,128)} collective-permute-done((f32[24,4096]{1,0:T(8,128)S(1)}, f32[24,4096]{1,0:T(8,128)}, u32[]{:S(2)}, u32[]{:S(2)}) %collective-permute-start.10) | collective-permute-done | bytes 393248 | tf_op jit(solution)/shard_map/ppermute | solution.py:39
  43.6 2.8 %collective-permute-start.14 = (f32[24,4096]{1,0:T(8,128)}, f32[24,4096]{1,0:T(8,128)}, u32[]{:S(2)}, u32[]{:S(2)}) collective-permute-start(f32[24,4096]{1,0:T(8,128)} %collective-permute-done.13.refs_14_), channel_id=1, source_target_pairs={{0,134},{1,135},{2,0},{3,1},{4,2},{5,3},{6,4},{7,5},{128,6},{129,7... | collective-permute-start | bytes 1179656 | tf_op jit(solution)/shard_map/ppermute | solution.py:39
  46.3 2.2 %collective-permute-done.17.refs_11_ = f32[48,4096]{1,0:T(8,128)S(1)} collective-permute-done((f32[48,4096]{1,0:T(8,128)S(1)}, f32[48,4096]{1,0:T(8,128)S(1)}, u32[]{:S(2)}, u32[]{:S(2)}) %collective-permute-start.17) | collective-permute-done | bytes 786464 | tf_op jit(solution)/shard_map/ppermute | solution.py:39
  48.5 0.8 slice.94
  49.3 0.8 slice.95
  50.1 2.7 %collective-permute-start.20 = (f32[24,4096]{1,0:T(8,128)}, f32[24,4096]{1,0:T(8,128)}, u32[]{:S(2)}, u32[]{:S(2)}) collective-permute-start(f32[24,4096]{1,0:T(8,128)} %slice.95), channel_id=1, source_target_pairs={{0,24},{1,25},{2,26},{3,27},{4,28},{5,29},{6,30},{7,31},{128,152},... | collective-permute-start | bytes 1179656 | tf_op jit(solution)/shard_map/ppermute | solution.py:39
  52.7 1.6 %collective-permute-start.12 = (f32[24,4096]{1,0:T(8,128)}, f32[24,4096]{1,0:T(8,128)S(1)}, u32[]{:S(2)}, u32[]{:S(2)}) collective-permute-start(f32[24,4096]{1,0:T(8,128)} %collective-permute-done.11.refs_12_), channel_id=1, source_target_pairs={{0,2},{1,3},{2,4},{3,5},{4,6},{5,7},{6,128},{7,129},{128,130},{129... | collective-permute-start | bytes 1179656 | tf_op jit(solution)/shard_map/ppermute | solution.py:39
  54.4 1.3 collective-permute-start.15
  55.7 2.0 %collective-permute-done.19.refs_13_ = f32[24,4096]{1,0:T(8,128)} collective-permute-done((f32[24,4096]{1,0:T(8,128)}, f32[24,4096]{1,0:T(8,128)}, u32[]{:S(2)}, u32[]{:S(2)}) %collective-permute-start.19) | collective-permute-done | bytes 393248 | tf_op jit(solution)/shard_map/ppermute | solution.py:39
  57.8 0.9 copy-done.2
  58.7 0.9 copy-done.4
  59.7 0.9 copy-done.6
  60.6 0.9 copy-done.8
  61.6 0.9 copy-done.10
  62.5 0.9 copy-done.12
  63.5 0.9 copy-done.14
  64.4 8.9 %first_half.1.refs_19_ = f32[2,32,8,256]{3,2,1,0:T(8,128)S(1)} custom-call(f32[16,8192]{1,0:T(8,128)S(1)} %reshape.67.refs_0_.refs_8_, f32[16,8192]{1,0:T(8,128)S(1)} %collective-permute-done.refs_1_, f32[16,8192]{1,0:T(8,128)S(1)} %collective-permute-done.1.refs_2_, f32[8,8192]{1,0:T(8,128)S(1)} %copy-done.8, f32[8,8192]{1,0:T(8,128)S(1)} %copy-done.10, ...), custom_call_target="tpu_custom_call" | custom-call | flops 3221225472 | bytes 12582912 | tf_op jit(solution)/shard_map/first_half/pallas_call | solution.py:255
  73.3 10.0 %second_half.1 = (f32[4,2,8,256]{3,2,1,0:T(8,128)S(1)}, f32[4,2,8,256]{3,2,1,0:T(8,128)S(1)}, f32[4,2,8,256]{3,2,1,0:T(8,128)S(1)}, f32[4,2,8,256]{3,2,1,0:T(8,1...) custom-call(s32[4]{0:T(128)S(1)} %pad_add_fusion.place, ...), custom_call_target="tpu_custom_call" | custom-call | flops 3221225472 | bytes 12582912 | tf_op jit(solution)/shard_map/second_half/pallas_call | solution.py:267
  83.3 11.0 %all-to-all-start = ((f32[8,2,2,2,8,256]{5,4,3,2,1,0:T(8,128)}), f32[8,2,2,2,8,256]{5,4,3,2,1,0:T(8,128)S(1)}, u32[]{:S(2)}, u32[]{:S(2)}) async-start(f32[8,2,2,2,8,256]{5,4,3,2,1,0:T(8,128)} %get-tuple-element.41), calls=%async_computation | async-start | bytes 1048576 | tf_op jit(solution)/shard_map/all_to_all | solution.py:283
  94.4 2.3 %collective-permute-start.21 = (f32[4,2,8,256]{3,2,1,0:T(8,128)S(1)}, f32[4,2,8,256]{3,2,1,0:T(8,128)S(1)}, u32[]{:S(2)}, u32[]{:S(2)}) collective-permute-start(f32[4,2,8,256]{3,2,1,0:T(8,128)S(1)} %get-tuple-element.30), channel_id=1, source_target_pairs={{0,134},{1,135},{2,0},{3,1},{4,2},{5,3},{6,4},{7,5},{128,6},{129,7... | collective-permute-start | bytes 196616 | tf_op jit(solution)/shard_map/ppermute | solution.py:39
  97.2 3.1 %collective-permute-start.23 = (f32[4,2,8,256]{3,2,1,0:T(8,128)S(1)}, f32[4,2,8,256]{3,2,1,0:T(8,128)S(1)}, u32[]{:S(2)}, u32[]{:S(2)}) collective-permute-start(f32[4,2,8,256]{3,2,1,0:T(8,128)S(1)} %get-tuple-element.32), channel_id=1, source_target_pairs={{0,130},{1,131},{2,132},{3,133},{4,134},{5,135},{6,0},{7,1},{128,2... | collective-permute-start | bytes 196616 | tf_op jit(solution)/shard_map/ppermute | solution.py:39
  100.3 1.4 collective-permute-start.24
  101.7 2.1 %all-to-all-done.came = f32[8,2,2,2,8,256]{5,4,3,2,1,0:T(8,128)S(1)} async-done(((f32[8,2,2,2,8,256]{5,4,3,2,1,0:T(8,128)}), f32[8,2,2,2,8,256]{5,4,3,2,1,0:T(8,128)S(1)}, u32[]{:S(2)}, u32[]{:S(2)}) %all-to-all-start) | async-done | bytes 524320 | tf_op jit(solution)/shard_map/all_to_all | solution.py:283
  103.8 1.4 z_pack.1
  105.2 3.5 %collective-permute-start.26 = (f32[4,2,8,256]{3,2,1,0:T(8,128)S(1)}, f32[4,2,8,256]{3,2,1,0:T(8,128)S(1)}, u32[]{:S(2)}, u32[]{:S(2)}) collective-permute-start(f32[4,2,8,256]{3,2,1,0:T(8,128)S(1)} %get-tuple-element.36), channel_id=1, source_target_pairs={{0,6},{1,7},{2,128},{3,129},{4,130},{5,131},{6,132},{7,133},{128,1... | collective-permute-start | bytes 196616 | tf_op jit(solution)/shard_map/ppermute | solution.py:39
  109.5 2.0 %collective-permute-start.32 = (f32[2,2,2,8,256]{4,3,2,1,0:T(8,128)S(1)}, f32[2,2,2,8,256]{4,3,2,1,0:T(8,128)S(1)}, u32[]{:S(2)}, u32[]{:S(2)}) collective-permute-start(f32[2,2,2,8,256]{4,3,2,1,0:T(8,128)S(1)} %get-tuple-element.45), channel_id=1, source_target_pairs={{0,6},{1,7},{2,128},{3,129},{4,130},{5,131},{6,132},{7,133},{128,1... | collective-permute-start | bytes 196616 | tf_op jit(solution)/shard_map/ppermute | solution.py:39
  112.6 4.0 %collective-permute-start.33 = (f32[2,2,2,8,256]{4,3,2,1,0:T(8,128)}, f32[2,2,2,8,256]{4,3,2,1,0:T(8,128)}, u32[]{:S(2)}, u32[]{:S(2)}) collective-permute-start(f32[2,2,2,8,256]{4,3,2,1,0:T(8,128)} %get-tuple-element.46), channel_id=1, source_target_pairs={{0,128},{1,129},{2,130},{3,131},{4,132},{5,133},{6,134},{7,135},{1... | collective-permute-start | bytes 196616 | tf_op jit(solution)/shard_map/ppermute | solution.py:39
  117.3 1.7 %collective-permute-start.34 = (f32[2,2,2,8,256]{4,3,2,1,0:T(8,128)}, f32[2,2,2,8,256]{4,3,2,1,0:T(8,128)}, u32[]{:S(2)}, u32[]{:S(2)}) collective-permute-start(f32[2,2,2,8,256]{4,3,2,1,0:T(8,128)} %get-tuple-element.47), channel_id=1, source_target_pairs={{0,130},{1,131},{2,132},{3,133},{4,134},{5,135},{6,0},{7,1},{128,2... | collective-permute-start | bytes 196616 | tf_op jit(solution)/shard_map/ppermute | solution.py:39
  119.6 2.2 %collective-permute-start.35 = (f32[2,2,2,8,256]{4,3,2,1,0:T(8,128)}, f32[2,2,2,8,256]{4,3,2,1,0:T(8,128)}, u32[]{:S(2)}, u32[]{:S(2)}) collective-permute-start(f32[2,2,2,8,256]{4,3,2,1,0:T(8,128)} %get-tuple-element.48), channel_id=1, source_target_pairs={{0,132},{1,133},{2,134},{3,135},{4,0},{5,1},{6,2},{7,3},{128,4},{1... | collective-permute-start | bytes 196616 | tf_op jit(solution)/shard_map/ppermute | solution.py:39
  121.9 0.7 collective-permute-start.36
  123.3 1.4 reshape.68.refs_9_
  124.8 4.5 %collective-permute-start.28 = (f32[8,2,8,256]{3,2,1,0:T(8,128)}, f32[8,2,8,256]{3,2,1,0:T(8,128)}, u32[]{:S(2)}, u32[]{:S(2)}) collective-permute-start(f32[8,2,8,256]{3,2,1,0:T(8,128)} %copy-done.26), channel_id=1, source_target_pairs={{0,16},{1,17},{2,18},{3,19},{4,20},{5,21},{6,22},{7,23},{128,144},... | collective-permute-start | bytes 393224 | tf_op jit(solution)/shard_map/ppermute | solution.py:39
  129.3 2.1 %collective-permute-done.36.refs_7_ = f32[2,2,2,8,256]{4,3,2,1,0:T(8,128)} collective-permute-done((f32[2,2,2,8,256]{4,3,2,1,0:T(8,128)}, f32[2,2,2,8,256]{4,3,2,1,0:T(8,128)}, u32[]{:S(2)}, u32[]{:S(2)}) %collective-permute-start.36) | collective-permute-done | bytes 65568 | tf_op jit(solution)/shard_map/ppermute | solution.py:39
  131.4 0.8 copy-done.20
  132.3 0.8 copy-done.22
  133.1 0.8 copy-done.24
  134.0 2.0 %y_pack.1 = (f32[4,2,2,8,256]{4,3,2,1,0:T(8,128)S(1)}, f32[4,2,2,8,256]{4,3,2,1,0:T(8,128)}, f32[4,2,2,8,256]{4,3,2,1,0:T(8,128)}, f32[4,2,2,8,256]{4,3,2,1,0:T(8,128)}) custom-call(s32[4]{0:T(128)S(1)} %pad_add_fusion.place, f32[2,2,2,8,256]{4,3,2,1,0:T(8,128)S(1)} %get-tuple-element.42.refs_0_, f32[2,2,2,8,256]{4,3,2,1,0:T(8,128)S(1)} %copy-done.20, ...), custom_call_target="tpu_custom_call" | custom-call | tf_op jit(solution)/shard_map/y_pack/pallas_call | solution.py:306
  136.6 0.9 collective-permute-start.37
  137.5 3.4 %collective-permute-start.38 = (f32[4,2,2,8,256]{4,3,2,1,0:T(8,128)}, f32[4,2,2,8,256]{4,3,2,1,0:T(8,128)}, u32[]{:S(2)}, u32[]{:S(2)}) collective-permute-start(f32[4,2,2,8,256]{4,3,2,1,0:T(8,128)} %get-tuple-element.52), channel_id=1, source_target_pairs={{0,16},{1,17},{2,18},{3,19},{4,20},{5,21},{6,22},{7,23},{128,144},... | collective-permute-start | bytes 393224 | tf_op jit(solution)/shard_map/ppermute | solution.py:39
  141.0 2.1 %collective-permute-start.39 = (f32[4,2,2,8,256]{4,3,2,1,0:T(8,128)}, f32[4,2,2,8,256]{4,3,2,1,0:T(8,128)}, u32[]{:S(2)}, u32[]{:S(2)}) collective-permute-start(f32[4,2,2,8,256]{4,3,2,1,0:T(8,128)} %get-tuple-element.53), channel_id=1, source_target_pairs={{0,24},{1,25},{2,26},{3,27},{4,28},{5,29},{6,30},{7,31},{128,152},... | collective-permute-start | bytes 393224 | tf_op jit(solution)/shard_map/ppermute | solution.py:39
  143.1 0.8 broadcast_add_fusion
  143.8 1.0 add.77.refs_10_
  144.9 2.0 %collective-permute-done.38.refs_6_ = f32[4,2,2,8,256]{4,3,2,1,0:T(8,128)} collective-permute-done((f32[4,2,2,8,256]{4,3,2,1,0:T(8,128)}, f32[4,2,2,8,256]{4,3,2,1,0:T(8,128)}, u32[]{:S(2)}, u32[]{:S(2)}) %collective-permute-start.38) | collective-permute-done | bytes 131104 | tf_op jit(solution)/shard_map/ppermute | solution.py:39
  146.9 0.9 copy-done.18
  147.8 2.4 %final.1 = (f32[16,8192]{1,0:T(8,128)S(1)}, f32[16,8192]{1,0:T(8,128)S(1)}) custom-call(s32[4]{0:T(128)S(1)} %pad_add_fusion.place, f32[8,2,8,256]{3,2,1,0:T(8,128)S(1)} %get-tuple-element.37.refs_0_, f32[8,2,8,256]{3,2,1,0:T(8,128)S(1)} %collective-permute-done.27.refs_1_, f32[8,2,8,256]{3,2,1,0:T(8,128)} %collective-permute-done.28.refs_2_, ...), custom_call_target="tpu_custom_call" | custom-call | tf_op jit(solution)/shard_map/final/pallas_call | solution.py:326
  150.2 0.8 copy-done.15
  151.1 0.8 copy-done.16
  151.9 2.1 %reshape.69 = f32[8,2,8192]{2,1,0:T(2,128)} reshape(f32[16,8192]{1,0:T(8,128)} %copy-done.16) | data formatting | bytes 1048576 | tf_op jit(solution)/shard_map/reshape | solution.py:337
  154.0 2.1 %reshape.70 = f32[8,2,8192]{2,1,0:T(2,128)} reshape(f32[16,8192]{1,0:T(8,128)} %copy-done.15) | data formatting | bytes 1048576 | tf_op jit(solution)/shard_map/reshape | solution.py:337
  (118 shorter events, 8.2 us)
Async XLA Ops:
  0.6 122.0 %copy-start = (f32[256]{0:T(256)S(1)}, f32[256]{0:T(256)}, u32[]{:S(2)}) copy-start(f32[256]{0:T(256)} %param.10) | copy-start | bytes 3076
  1.9 12.5 %collective-permute-start.4 = (f32[8,8192]{1,0:T(8,128)S(1)}, f32[8,8192]{1,0:T(8,128)S(1)}, u32[]{:S(2)}, u32[]{:S(2)}) collective-permute-start(f32[8,8192]{1,0:T(8,128)S(1)} %slice.63), channel_id=1, source_target_pairs={{0,2},{1,3},{2,4},{3,5},{4,6},{5,7},{6,128},{7,129},{128,130},{129... | collective-permute-start | bytes 786440 | tf_op jit(solution)/shard_map/ppermute | solution.py:39
  5.9 15.0 %collective-permute-start = (f32[16,8192]{1,0:T(8,128)S(1)}, f32[16,8192]{1,0:T(8,128)S(1)}, u32[]{:S(2)}, u32[]{:S(2)}) collective-permute-start(f32[16,8192]{1,0:T(8,128)S(1)} %reshape.67.refs_0_.refs_8_), channel_id=1, source_target_pairs={{0,8},{1,9},{2,10},{3,11},{4,12},{5,13},{6,14},{7,15},{128,136},{1... | collective-permute-start | bytes 1572872 | tf_op jit(solution)/shard_map/ppermute | solution.py:39
  7.2 13.8 %collective-permute-start.1 = (f32[16,8192]{1,0:T(8,128)S(1)}, f32[16,8192]{1,0:T(8,128)S(1)}, u32[]{:S(2)}, u32[]{:S(2)}) collective-permute-start(f32[16,8192]{1,0:T(8,128)S(1)} %reshape.67.refs_0_.refs_8_), channel_id=1, source_target_pairs={{0,24},{1,25},{2,26},{3,27},{4,28},{5,29},{6,30},{7,31},{128,152},... | collective-permute-start | bytes 1572872 | tf_op jit(solution)/shard_map/ppermute | solution.py:39
  8.9 8.5 %collective-permute-start.7 = (f32[8,8192]{1,0:T(8,128)S(1)}, f32[8,8192]{1,0:T(8,128)S(1)}, u32[]{:S(2)}, u32[]{:S(2)}) collective-permute-start(f32[8,8192]{1,0:T(8,128)S(1)} %slice.65), channel_id=1, source_target_pairs={{0,134},{1,135},{2,0},{3,1},{4,2},{5,3},{6,4},{7,5},{128,6},{129,7... | collective-permute-start | bytes 786440 | tf_op jit(solution)/shard_map/ppermute | solution.py:39
  13.0 44.8 %collective-permute-start.16 = (f32[256,8192]{1,0:T(8,128)}, f32[256,8192]{1,0:T(8,128)}, u32[]{:S(2)}, u32[]{:S(2)}) collective-permute-start(f32[256,8192]{1,0:T(8,128)} %refs_17_.1), channel_id=1, source_target_pairs={{0,1},{1,0},{2,3},{3,2},{4,5},{5,4},{6,7},{7,6},{128,129},{129,128... | collective-permute-start | bytes 25165832 | tf_op jit(solution)/shard_map/ppermute | solution.py:39
  14.4 9.4 %collective-permute-start.5 = (f32[8,8192]{1,0:T(8,128)S(1)}, f32[8,8192]{1,0:T(8,128)S(1)}, u32[]{:S(2)}, u32[]{:S(2)}) collective-permute-start(f32[8,8192]{1,0:T(8,128)S(1)} %collective-permute-done.4.refs_5_), channel_id=1, source_target_pairs={{0,2},{1,3},{2,4},{3,5},{4,6},{5,7},{6,128},{7,129},{128,130},{129... | collective-permute-start | bytes 786440 | tf_op jit(solution)/shard_map/ppermute | solution.py:39
  17.5 13.7 %copy-start.1 = (f32[8,8192]{1,0:T(8,128)}, f32[8,8192]{1,0:T(8,128)S(1)}, u32[]{:S(2)}) copy-start(f32[8,8192]{1,0:T(8,128)S(1)} %collective-permute-done.7.refs_8_) | copy-start | bytes 786436
  17.5 7.0 %collective-permute-start.8 = (f32[8,8192]{1,0:T(8,128)S(1)}, f32[8,8192]{1,0:T(8,128)S(1)}, u32[]{:S(2)}, u32[]{:S(2)}) collective-permute-start(f32[8,8192]{1,0:T(8,128)S(1)} %collective-permute-done.7.refs_8_), channel_id=1, source_target_pairs={{0,134},{1,135},{2,0},{3,1},{4,2},{5,3},{6,4},{7,5},{128,6},{129,7... | collective-permute-start | bytes 786440 | tf_op jit(solution)/shard_map/ppermute | solution.py:39
  20.9 13.7 %collective-permute-start.2 = (f32[8,8192]{1,0:T(8,128)S(1)}, f32[8,8192]{1,0:T(8,128)S(1)}, u32[]{:S(2)}, u32[]{:S(2)}) collective-permute-start(f32[8,8192]{1,0:T(8,128)S(1)} %slice.80), channel_id=1, source_target_pairs={{0,8},{1,9},{2,10},{3,11},{4,12},{5,13},{6,14},{7,15},{128,136},{1... | collective-permute-start | bytes 786440 | tf_op jit(solution)/shard_map/ppermute | solution.py:39
  21.0 15.2 %collective-permute-start.3 = (f32[8,8192]{1,0:T(8,128)S(1)}, f32[8,8192]{1,0:T(8,128)S(1)}, u32[]{:S(2)}, u32[]{:S(2)}) collective-permute-start(f32[8,8192]{1,0:T(8,128)S(1)} %slice.81), channel_id=1, source_target_pairs={{0,24},{1,25},{2,26},{3,27},{4,28},{5,29},{6,30},{7,31},{128,152},... | collective-permute-start | bytes 786440 | tf_op jit(solution)/shard_map/ppermute | solution.py:39
  23.8 7.4 %copy-start.3 = (f32[8,8192]{1,0:T(8,128)}, f32[8,8192]{1,0:T(8,128)S(1)}, u32[]{:S(2)}) copy-start(f32[8,8192]{1,0:T(8,128)S(1)} %collective-permute-done.5.refs_6_) | copy-start | bytes 786436
  23.8 6.9 %collective-permute-start.6 = (f32[8,8192]{1,0:T(8,128)S(1)}, f32[8,8192]{1,0:T(8,128)S(1)}, u32[]{:S(2)}, u32[]{:S(2)}) collective-permute-start(f32[8,8192]{1,0:T(8,128)S(1)} %collective-permute-done.5.refs_6_), channel_id=1, source_target_pairs={{0,2},{1,3},{2,4},{3,5},{4,6},{5,7},{6,128},{7,129},{128,130},{129... | collective-permute-start | bytes 786440 | tf_op jit(solution)/shard_map/ppermute | solution.py:39
  24.5 6.7 %copy-start.5 = (f32[8,8192]{1,0:T(8,128)}, f32[8,8192]{1,0:T(8,128)S(1)}, u32[]{:S(2)}) copy-start(f32[8,8192]{1,0:T(8,128)S(1)} %collective-permute-done.8.refs_9_) | copy-start | bytes 786436
  24.5 6.7 %collective-permute-start.9 = (f32[8,8192]{1,0:T(8,128)S(1)}, f32[8,8192]{1,0:T(8,128)S(1)}, u32[]{:S(2)}, u32[]{:S(2)}) collective-permute-start(f32[8,8192]{1,0:T(8,128)S(1)} %collective-permute-done.8.refs_9_), channel_id=1, source_target_pairs={{0,134},{1,135},{2,0},{3,1},{4,2},{5,3},{6,4},{7,5},{128,6},{129,7... | collective-permute-start | bytes 786440 | tf_op jit(solution)/shard_map/ppermute | solution.py:39
  31.9 16.6 %collective-permute-start.17 = (f32[48,4096]{1,0:T(8,128)S(1)}, f32[48,4096]{1,0:T(8,128)S(1)}, u32[]{:S(2)}, u32[]{:S(2)}) collective-permute-start(f32[48,4096]{1,0:T(8,128)S(1)} %slice_dynamic-update-slice_fusion), channel_id=1, source_target_pairs={{0,8},{1,9},{2,10},{3,11},{4,12},{5,13},{6,14},{7,15},{128,136},{1... | collective-permute-start | bytes 2359304 | tf_op jit(solution)/shard_map/ppermute | solution.py:39
  31.9 17.3 %collective-permute-start.18 = (f32[48,4096]{1,0:T(8,128)S(1)}, f32[48,4096]{1,0:T(8,128)S(1)}, u32[]{:S(2)}, u32[]{:S(2)}) collective-permute-start(f32[48,4096]{1,0:T(8,128)S(1)} %slice_dynamic-update-slice_fusion), channel_id=1, source_target_pairs={{0,24},{1,25},{2,26},{3,27},{4,28},{5,29},{6,30},{7,31},{128,152},... | collective-permute-start | bytes 2359304 | tf_op jit(solution)/shard_map/ppermute | solution.py:39
  34.6 14.7 %copy-start.7 = (f32[8,8192]{1,0:T(8,128)}, f32[8,8192]{1,0:T(8,128)S(1)}, u32[]{:S(2)}) copy-start(f32[8,8192]{1,0:T(8,128)S(1)} %collective-permute-done.2.refs_3_) | copy-start | bytes 786436
  34.7 8.7 %collective-permute-start.10 = (f32[24,4096]{1,0:T(8,128)S(1)}, f32[24,4096]{1,0:T(8,128)}, u32[]{:S(2)}, u32[]{:S(2)}) collective-permute-start(f32[24,4096]{1,0:T(8,128)S(1)} %pad_maximum_fusion), channel_id=1, source_target_pairs={{0,2},{1,3},{2,4},{3,5},{4,6},{5,7},{6,128},{7,129},{128,130},{129... | collective-permute-start | bytes 1179656 | tf_op jit(solution)/shard_map/ppermute | solution.py:39
  36.2 13.8 %copy-start.9 = (f32[8,8192]{1,0:T(8,128)}, f32[8,8192]{1,0:T(8,128)S(1)}, u32[]{:S(2)}) copy-start(f32[8,8192]{1,0:T(8,128)S(1)} %collective-permute-done.3.refs_4_) | copy-start | bytes 786436
  36.3 7.3 %collective-permute-start.13 = (f32[24,4096]{1,0:T(8,128)S(1)}, f32[24,4096]{1,0:T(8,128)}, u32[]{:S(2)}, u32[]{:S(2)}) collective-permute-start(f32[24,4096]{1,0:T(8,128)S(1)} %pad_maximum_fusion.1), channel_id=1, source_target_pairs={{0,134},{1,135},{2,0},{3,1},{4,2},{5,3},{6,4},{7,5},{128,6},{129,7... | collective-permute-start | bytes 1179656 | tf_op jit(solution)/shard_map/ppermute | solution.py:39
  43.3 9.4 %collective-permute-start.11 = (f32[24,4096]{1,0:T(8,128)}, f32[24,4096]{1,0:T(8,128)}, u32[]{:S(2)}, u32[]{:S(2)}) collective-permute-start(f32[24,4096]{1,0:T(8,128)} %collective-permute-done.10.refs_11_), channel_id=1, source_target_pairs={{0,2},{1,3},{2,4},{3,5},{4,6},{5,7},{6,128},{7,129},{128,130},{129... | collective-permute-start | bytes 1179656 | tf_op jit(solution)/shard_map/ppermute | solution.py:39
  43.6 10.8 %collective-permute-start.14 = (f32[24,4096]{1,0:T(8,128)}, f32[24,4096]{1,0:T(8,128)}, u32[]{:S(2)}, u32[]{:S(2)}) collective-permute-start(f32[24,4096]{1,0:T(8,128)} %collective-permute-done.13.refs_14_), channel_id=1, source_target_pairs={{0,134},{1,135},{2,0},{3,1},{4,2},{5,3},{6,4},{7,5},{128,6},{129,7... | collective-permute-start | bytes 1179656 | tf_op jit(solution)/shard_map/ppermute | solution.py:39
  49.3 8.4 %collective-permute-start.19 = (f32[24,4096]{1,0:T(8,128)}, f32[24,4096]{1,0:T(8,128)}, u32[]{:S(2)}, u32[]{:S(2)}) collective-permute-start(f32[24,4096]{1,0:T(8,128)} %slice.94), channel_id=1, source_target_pairs={{0,8},{1,9},{2,10},{3,11},{4,12},{5,13},{6,14},{7,15},{128,136},{1... | collective-permute-start | bytes 1179656 | tf_op jit(solution)/shard_map/ppermute | solution.py:39
  50.1 7.7 %collective-permute-start.20 = (f32[24,4096]{1,0:T(8,128)}, f32[24,4096]{1,0:T(8,128)}, u32[]{:S(2)}, u32[]{:S(2)}) collective-permute-start(f32[24,4096]{1,0:T(8,128)} %slice.95), channel_id=1, source_target_pairs={{0,24},{1,25},{2,26},{3,27},{4,28},{5,29},{6,30},{7,31},{128,152},... | collective-permute-start | bytes 1179656 | tf_op jit(solution)/shard_map/ppermute | solution.py:39
  52.7 20.6 %collective-permute-start.12 = (f32[24,4096]{1,0:T(8,128)}, f32[24,4096]{1,0:T(8,128)S(1)}, u32[]{:S(2)}, u32[]{:S(2)}) collective-permute-start(f32[24,4096]{1,0:T(8,128)} %collective-permute-done.11.refs_12_), channel_id=1, source_target_pairs={{0,2},{1,3},{2,4},{3,5},{4,6},{5,7},{6,128},{7,129},{128,130},{129... | collective-permute-start | bytes 1179656 | tf_op jit(solution)/shard_map/ppermute | solution.py:39
  54.4 18.9 %collective-permute-start.15 = (f32[24,4096]{1,0:T(8,128)}, f32[24,4096]{1,0:T(8,128)S(1)}, u32[]{:S(2)}, u32[]{:S(2)}) collective-permute-start(f32[24,4096]{1,0:T(8,128)} %collective-permute-done.14.refs_15_), channel_id=1, source_target_pairs={{0,134},{1,135},{2,0},{3,1},{4,2},{5,3},{6,4},{7,5},{128,6},{129,7... | collective-permute-start | bytes 1179656 | tf_op jit(solution)/shard_map/ppermute | solution.py:39
  57.8 1.0 copy-start.2
  58.7 0.9 copy-start.4
  59.7 0.9 copy-start.6
  60.6 0.9 copy-start.8
  61.6 0.9 copy-start.10
  62.5 0.9 copy-start.12
  63.5 0.9 copy-start.14
  83.3 39.3 %copy-start.27 = (s32[256]{0:T(256)S(1)}, s32[256]{0:T(256)}, u32[]{:S(2)}) copy-start(s32[256]{0:T(256)} %param.11) | copy-start | bytes 3076
  83.3 39.5 %copy-start.28 = (f32[64]{0:T(128)S(1)}, f32[64]{0:T(128)}, u32[]{:S(2)}) copy-start(f32[64]{0:T(128)} %param.9) | copy-start | bytes 772
  83.3 20.5 %all-to-all-start = ((f32[8,2,2,2,8,256]{5,4,3,2,1,0:T(8,128)}), f32[8,2,2,2,8,256]{5,4,3,2,1,0:T(8,128)S(1)}, u32[]{:S(2)}, u32[]{:S(2)}) async-start(f32[8,2,2,2,8,256]{5,4,3,2,1,0:T(8,128)} %get-tuple-element.41), calls=%async_computation | async-start | bytes 1048576 | tf_op jit(solution)/shard_map/all_to_all | solution.py:283
  94.4 10.8 %collective-permute-start.21 = (f32[4,2,8,256]{3,2,1,0:T(8,128)S(1)}, f32[4,2,8,256]{3,2,1,0:T(8,128)S(1)}, u32[]{:S(2)}, u32[]{:S(2)}) collective-permute-start(f32[4,2,8,256]{3,2,1,0:T(8,128)S(1)} %get-tuple-element.30), channel_id=1, source_target_pairs={{0,134},{1,135},{2,0},{3,1},{4,2},{5,3},{6,4},{7,5},{128,6},{129,7... | collective-permute-start | bytes 196616 | tf_op jit(solution)/shard_map/ppermute | solution.py:39
  96.6 12.1 %collective-permute-start.22 = (f32[4,2,8,256]{3,2,1,0:T(8,128)S(1)}, f32[4,2,8,256]{3,2,1,0:T(8,128)S(1)}, u32[]{:S(2)}, u32[]{:S(2)}) collective-permute-start(f32[4,2,8,256]{3,2,1,0:T(8,128)S(1)} %get-tuple-element.31), channel_id=1, source_target_pairs={{0,132},{1,133},{2,134},{3,135},{4,0},{5,1},{6,2},{7,3},{128,4},{1... | collective-permute-start | bytes 196616 | tf_op jit(solution)/shard_map/ppermute | solution.py:39
  97.2 11.7 %collective-permute-start.23 = (f32[4,2,8,256]{3,2,1,0:T(8,128)S(1)}, f32[4,2,8,256]{3,2,1,0:T(8,128)S(1)}, u32[]{:S(2)}, u32[]{:S(2)}) collective-permute-start(f32[4,2,8,256]{3,2,1,0:T(8,128)S(1)} %get-tuple-element.32), channel_id=1, source_target_pairs={{0,130},{1,131},{2,132},{3,133},{4,134},{5,135},{6,0},{7,1},{128,2... | collective-permute-start | bytes 196616 | tf_op jit(solution)/shard_map/ppermute | solution.py:39
  100.3 9.2 %collective-permute-start.24 = (f32[4,2,8,256]{3,2,1,0:T(8,128)S(1)}, f32[4,2,8,256]{3,2,1,0:T(8,128)S(1)}, u32[]{:S(2)}, u32[]{:S(2)}) collective-permute-start(f32[4,2,8,256]{3,2,1,0:T(8,128)S(1)} %get-tuple-element.34), channel_id=1, source_target_pairs={{0,2},{1,3},{2,4},{3,5},{4,6},{5,7},{6,128},{7,129},{128,130},{129... | collective-permute-start | bytes 196616 | tf_op jit(solution)/shard_map/ppermute | solution.py:39
  101.7 10.2 %collective-permute-start.25 = (f32[4,2,8,256]{3,2,1,0:T(8,128)}, f32[4,2,8,256]{3,2,1,0:T(8,128)S(1)}, u32[]{:S(2)}, u32[]{:S(2)}) collective-permute-start(f32[4,2,8,256]{3,2,1,0:T(8,128)} %get-tuple-element.35), channel_id=1, source_target_pairs={{0,4},{1,5},{2,6},{3,7},{4,128},{5,129},{6,130},{7,131},{128,132},... | collective-permute-start | bytes 196616 | tf_op jit(solution)/shard_map/ppermute | solution.py:39
  105.2 6.7 %collective-permute-start.26 = (f32[4,2,8,256]{3,2,1,0:T(8,128)S(1)}, f32[4,2,8,256]{3,2,1,0:T(8,128)S(1)}, u32[]{:S(2)}, u32[]{:S(2)}) collective-permute-start(f32[4,2,8,256]{3,2,1,0:T(8,128)S(1)} %get-tuple-element.36), channel_id=1, source_target_pairs={{0,6},{1,7},{2,128},{3,129},{4,130},{5,131},{6,132},{7,133},{128,1... | collective-permute-start | bytes 196616 | tf_op jit(solution)/shard_map/ppermute | solution.py:39
  108.7 8.0 %collective-permute-start.30 = (f32[2,2,2,8,256]{4,3,2,1,0:T(8,128)S(1)}, f32[2,2,2,8,256]{4,3,2,1,0:T(8,128)S(1)}, u32[]{:S(2)}, u32[]{:S(2)}) collective-permute-start(f32[2,2,2,8,256]{4,3,2,1,0:T(8,128)S(1)} %get-tuple-element.43), channel_id=1, source_target_pairs={{0,2},{1,3},{2,4},{3,5},{4,6},{5,7},{6,128},{7,129},{128,130},{129... | collective-permute-start | bytes 196616 | tf_op jit(solution)/shard_map/ppermute | solution.py:39
  108.9 10.1 %collective-permute-start.31 = (f32[2,2,2,8,256]{4,3,2,1,0:T(8,128)S(1)}, f32[2,2,2,8,256]{4,3,2,1,0:T(8,128)S(1)}, u32[]{:S(2)}, u32[]{:S(2)}) collective-permute-start(f32[2,2,2,8,256]{4,3,2,1,0:T(8,128)S(1)} %get-tuple-element.44), channel_id=1, source_target_pairs={{0,4},{1,5},{2,6},{3,7},{4,128},{5,129},{6,130},{7,131},{128,132},... | collective-permute-start | bytes 196616 | tf_op jit(solution)/shard_map/ppermute | solution.py:39
  109.5 12.4 %collective-permute-start.32 = (f32[2,2,2,8,256]{4,3,2,1,0:T(8,128)S(1)}, f32[2,2,2,8,256]{4,3,2,1,0:T(8,128)S(1)}, u32[]{:S(2)}, u32[]{:S(2)}) collective-permute-start(f32[2,2,2,8,256]{4,3,2,1,0:T(8,128)S(1)} %get-tuple-element.45), channel_id=1, source_target_pairs={{0,6},{1,7},{2,128},{3,129},{4,130},{5,131},{6,132},{7,133},{128,1... | collective-permute-start | bytes 196616 | tf_op jit(solution)/shard_map/ppermute | solution.py:39
  112.6 9.3 %copy-start.25 = (f32[8,2,8,256]{3,2,1,0:T(8,128)}, f32[8,2,8,256]{3,2,1,0:T(8,128)S(1)}, u32[]{:S(2)}) copy-start(f32[8,2,8,256]{3,2,1,0:T(8,128)S(1)} %get-tuple-element.40) | copy-start | bytes 393220
  112.6 9.3 %copy-start.26 = (f32[8,2,8,256]{3,2,1,0:T(8,128)}, f32[8,2,8,256]{3,2,1,0:T(8,128)S(1)}, u32[]{:S(2)}) copy-start(f32[8,2,8,256]{3,2,1,0:T(8,128)S(1)} %get-tuple-element.39) | copy-start | bytes 393220
  112.6 28.4 %collective-permute-start.27 = (f32[8,2,8,256]{3,2,1,0:T(8,128)}, f32[8,2,8,256]{3,2,1,0:T(8,128)S(1)}, u32[]{:S(2)}, u32[]{:S(2)}) collective-permute-start(f32[8,2,8,256]{3,2,1,0:T(8,128)} %get-tuple-element.38), channel_id=1, source_target_pairs={{0,8},{1,9},{2,10},{3,11},{4,12},{5,13},{6,14},{7,15},{128,136},{1... | collective-permute-start | bytes 393224 | tf_op jit(solution)/shard_map/ppermute | solution.py:39
  112.6 12.2 %collective-permute-start.33 = (f32[2,2,2,8,256]{4,3,2,1,0:T(8,128)}, f32[2,2,2,8,256]{4,3,2,1,0:T(8,128)}, u32[]{:S(2)}, u32[]{:S(2)}) collective-permute-start(f32[2,2,2,8,256]{4,3,2,1,0:T(8,128)} %get-tuple-element.46), channel_id=1, source_target_pairs={{0,128},{1,129},{2,130},{3,131},{4,132},{5,133},{6,134},{7,135},{1... | collective-permute-start | bytes 196616 | tf_op jit(solution)/shard_map/ppermute | solution.py:39
  117.3 12.0 %collective-permute-start.34 = (f32[2,2,2,8,256]{4,3,2,1,0:T(8,128)}, f32[2,2,2,8,256]{4,3,2,1,0:T(8,128)}, u32[]{:S(2)}, u32[]{:S(2)}) collective-permute-start(f32[2,2,2,8,256]{4,3,2,1,0:T(8,128)} %get-tuple-element.47), channel_id=1, source_target_pairs={{0,130},{1,131},{2,132},{3,133},{4,134},{5,135},{6,0},{7,1},{128,2... | collective-permute-start | bytes 196616 | tf_op jit(solution)/shard_map/ppermute | solution.py:39
  119.6 9.7 %collective-permute-start.35 = (f32[2,2,2,8,256]{4,3,2,1,0:T(8,128)}, f32[2,2,2,8,256]{4,3,2,1,0:T(8,128)}, u32[]{:S(2)}, u32[]{:S(2)}) collective-permute-start(f32[2,2,2,8,256]{4,3,2,1,0:T(8,128)} %get-tuple-element.48), channel_id=1, source_target_pairs={{0,132},{1,133},{2,134},{3,135},{4,0},{5,1},{6,2},{7,3},{128,4},{1... | collective-permute-start | bytes 196616 | tf_op jit(solution)/shard_map/ppermute | solution.py:39
  121.9 1.4 copy-start.23
  121.9 9.6 %collective-permute-start.36 = (f32[2,2,2,8,256]{4,3,2,1,0:T(8,128)}, f32[2,2,2,8,256]{4,3,2,1,0:T(8,128)}, u32[]{:S(2)}, u32[]{:S(2)}) collective-permute-start(f32[2,2,2,8,256]{4,3,2,1,0:T(8,128)} %get-tuple-element.49), channel_id=1, source_target_pairs={{0,134},{1,135},{2,0},{3,1},{4,2},{5,3},{6,4},{7,5},{128,6},{129,7... | collective-permute-start | bytes 196616 | tf_op jit(solution)/shard_map/ppermute | solution.py:39
  124.8 20.0 %collective-permute-start.28 = (f32[8,2,8,256]{3,2,1,0:T(8,128)}, f32[8,2,8,256]{3,2,1,0:T(8,128)}, u32[]{:S(2)}, u32[]{:S(2)}) collective-permute-start(f32[8,2,8,256]{3,2,1,0:T(8,128)} %copy-done.26), channel_id=1, source_target_pairs={{0,16},{1,17},{2,18},{3,19},{4,20},{5,21},{6,22},{7,23},{128,144},... | collective-permute-start | bytes 393224 | tf_op jit(solution)/shard_map/ppermute | solution.py:39
  129.3 15.5 %collective-permute-start.29 = (f32[8,2,8,256]{3,2,1,0:T(8,128)}, f32[8,2,8,256]{3,2,1,0:T(8,128)}, u32[]{:S(2)}, u32[]{:S(2)}) collective-permute-start(f32[8,2,8,256]{3,2,1,0:T(8,128)} %copy-done.25), channel_id=1, source_target_pairs={{0,24},{1,25},{2,26},{3,27},{4,28},{5,29},{6,30},{7,31},{128,152},... | collective-permute-start | bytes 393224 | tf_op jit(solution)/shard_map/ppermute | solution.py:39
  131.4 0.8 copy-start.20
  132.3 0.8 copy-start.22
  133.1 0.8 copy-start.24
  136.6 8.3 %collective-permute-start.37 = (f32[4,2,2,8,256]{4,3,2,1,0:T(8,128)}, f32[4,2,2,8,256]{4,3,2,1,0:T(8,128)}, u32[]{:S(2)}, u32[]{:S(2)}) collective-permute-start(f32[4,2,2,8,256]{4,3,2,1,0:T(8,128)} %get-tuple-element.51), channel_id=1, source_target_pairs={{0,8},{1,9},{2,10},{3,11},{4,12},{5,13},{6,14},{7,15},{128,136},{1... | collective-permute-start | bytes 393224 | tf_op jit(solution)/shard_map/ppermute | solution.py:39
  137.5 9.3 %collective-permute-start.38 = (f32[4,2,2,8,256]{4,3,2,1,0:T(8,128)}, f32[4,2,2,8,256]{4,3,2,1,0:T(8,128)}, u32[]{:S(2)}, u32[]{:S(2)}) collective-permute-start(f32[4,2,2,8,256]{4,3,2,1,0:T(8,128)} %get-tuple-element.52), channel_id=1, source_target_pairs={{0,16},{1,17},{2,18},{3,19},{4,20},{5,21},{6,22},{7,23},{128,144},... | collective-permute-start | bytes 393224 | tf_op jit(solution)/shard_map/ppermute | solution.py:39
  141.0 5.9 %collective-permute-start.39 = (f32[4,2,2,8,256]{4,3,2,1,0:T(8,128)}, f32[4,2,2,8,256]{4,3,2,1,0:T(8,128)}, u32[]{:S(2)}, u32[]{:S(2)}) collective-permute-start(f32[4,2,2,8,256]{4,3,2,1,0:T(8,128)} %get-tuple-element.53), channel_id=1, source_target_pairs={{0,24},{1,25},{2,26},{3,27},{4,28},{5,29},{6,30},{7,31},{128,152},... | collective-permute-start | bytes 393224 | tf_op jit(solution)/shard_map/ppermute | solution.py:39
  146.9 0.9 copy-start.18
  150.2 0.8 copy-start.15
  (6 other events, 4.1 us)

commit v3 on v0

v3 whole, which is shorter than its diff:
```python
import jax
import jax.numpy as jnp
from jax import lax
from jax.experimental import pallas as pl
from jax.experimental.pallas import tpu as pltpu
from jax.sharding import PartitionSpec as P

NV = 256
IRREPS = 8
VH = 32
NP = 8192
HALF = NP // 2
TILE = 1024
ROWS = 256
COLS = 256
BOTH = ("ia", "ja")
F32 = jnp.float32
BF16 = jnp.bfloat16
MULTIPLY_LIMIT = 12


def device_at(x, y, z, c):
    z = z % 8
    return (z // 4 * 4 + x % 4) * 32 + (y % 4) * 8 + (z % 4) * 2 + c % 2


def moved(dx=0, dy=0, dz=0, dc=0):
    return [
        (device_at(x, y, z, c), device_at(x + dx, y + dy, z + dz, c + dc))
        for x in range(4)
        for y in range(4)
        for z in range(8)
        for c in range(2)
    ]


def shift(array, **steps):
    return lax.ppermute(array, BOTH, moved(**steps))


def split(value):
    high = value.astype(BF16)
    return high, (value - high.astype(F32)).astype(BF16)


def multiply(pieces, shifts, own, partner, offset, total):
    dims = (((1,), (1,)), ((), ()))
    total[...] = jnp.zeros_like(total)

    def tile(k, carry):
        def columns(start):
            return pl.ds(pl.multiple_of(k * TILE + start, TILE), TILE)

        parts = [piece[:, columns(start)] for piece, start in zip(pieces, shifts)]
        t_high, t_low = split(jnp.concatenate(parts, axis=0))
        at = columns(offset)
        v_high, v_low = split(jnp.concatenate([own[:, at], partner[:, at]], axis=0))
        part = lax.dot_general(t_high, v_low, dims, preferred_element_type=F32)
        part += lax.dot_general(t_low, v_high, dims, preferred_element_type=F32)
        part += lax.dot_general(t_high, v_high, dims, preferred_element_type=F32)
        total[...] += part
        return carry

    lax.fori_loop(0, HALF // TILE, tile, 0)


def prepare_kernel(order, energy, pair, turn):
    row = lax.broadcasted_iota(jnp.int32, (NV, NV), 0)
    chosen = (row == order[...]).astype(BF16)
    values, dims = energy[...], (((1,), (0,)), ((), ()))
    grouped = exact(values, chosen, dims)
    lane = lax.broadcasted_iota(jnp.int32, (IRREPS, NV), 1)
    irrep = lax.broadcasted_iota(jnp.int32, (IRREPS, NV), 0)
    spread = jnp.where(lane // VH == irrep, jnp.broadcast_to(grouped, (IRREPS, NV)), 0.0)
    orbital = lax.broadcasted_iota(jnp.int32, (NV, VH * VH), 0) % VH
    spot = lax.broadcasted_iota(jnp.int32, (NV, VH * VH), 1)
    both = (spot // VH == orbital).astype(F32) + (spot % VH == orbital).astype(F32)
    pair[...] = exact(spread, both.astype(BF16), dims)
    old = lax.broadcasted_iota(jnp.int32, (VH * VH, VH * VH), 0)
    new = lax.broadcasted_iota(jnp.int32, (VH * VH, VH * VH), 1)
    turn[...] = (new == old % VH * VH + old // VH).astype(BF16)


def exact(value, whole, dims):
    high = value.astype(BF16)
    rest = value - high.astype(F32)
    middle = rest.astype(BF16)
    low = (rest - middle.astype(F32)).astype(BF16)
    result = lax.dot_general(high, whole, dims, preferred_element_type=F32)
    result += lax.dot_general(middle, whole, dims, preferred_element_type=F32)
    return result + lax.dot_general(low, whole, dims, preferred_element_type=F32)


def relayout_kernel(rows, own, up, down):
    value = rows[...].reshape(16, NP)
    own[...] = value
    up[...] = value[:8]
    down[...] = value[8:]


def touch_kernel(own, partner, mark):
    mark[...] = jnp.zeros_like(mark)


def low_pack_kernel(*refs):
    for n in range(6):
        refs[6][n * 8 : n * 8 + 8, :] = refs[n][:, :HALF]


def high_pack_kernel(below, above, far_up, far_down, up, down):
    up[:8, :] = below[:8, HALF:]
    up[8:16, :] = above[:8, HALF:]
    up[16:, :] = far_up[:, HALF:]
    down[:8, :] = below[8:, HALF:]
    down[8:16, :] = above[8:, HALF:]
    down[16:, :] = far_down[:, HALF:]


def spot():
    ia, ja = lax.axis_index("ia"), lax.axis_index("ja")
    z = ia // 4 * 4 + lax.rem(ja // 2, 4)
    return lax.rem(ia, 4), ja // 8, z, lax.rem(ja, 2)


def slot_of(dy, side, dz):
    return dy * 8 + side * 4 + dz


def first_half_kernel(slots, *refs):
    count = len(refs) - 4
    own, partner, out, total = refs[count:]
    multiply(refs[:count], [0] * count, own, partner, 0, total)
    for block, slot in enumerate(slots):
        for v in range(2):
            out[v, slot] = total[block * 8 : block * 8 + 8, v * COLS : (v + 1) * COLS]


def second_half_kernel(slots, near, *refs):
    count = len(refs) - 13
    own, partner, first = refs[count : count + 3]
    direct, crossed = refs[count + 3 : count + 7], refs[count + 7 : count + 11]
    total, sums = refs[count + 11 :]
    shifts = [HALF] * near + [0] * (count - near)
    multiply(refs[:count], shifts, own, partner, HALF, total)
    for block, slot in enumerate(slots):
        dy, at = slot // 8, slot % 8
        for v in range(2):
            value = first[v, slot] + total[block * 8 : block * 8 + 8, v * COLS : (v + 1) * COLS]
            sums[v, slot] = value
            direct[dy][at, v] = value
    x, y, z, c = spot()
    for dx in range(4):
        to = lax.rem(x + dx, 4)
        for k in range(2):
            for m in range(2):
                z_low = lax.rem(to, 2) * 2 + m
                dy = lax.rem(2 * k + to // 2 - y + 4, 4)
                up = dy * 8 + lax.rem(z - z_low + 4, 4)
                down = dy * 8 + 4 + lax.rem(z_low - z + 8, 4)
                for core in range(2):
                    v = lax.rem(c + core, 2)
                    a, b = sums[v, up], sums[v, down]
                    crossed[dx][k, m, core, 0] = jnp.concatenate([a[:4], b[:4]], axis=0)
                    crossed[dx][k, m, core, 1] = jnp.concatenate([a[4:], b[4:]], axis=0)


def z_pack_kernel(*refs):
    came, direct, outs, home, held = refs[:4], refs[4:8], refs[8:16], refs[16], refs[17]
    x, y, z, c = spot()
    for dx in range(4):
        held[dx] = came[dx][...]
    for dy in range(4):
        home[0, dy] = direct[dy][0]
        home[1, dy] = direct[dy][4]
    for d in range(8):
        to = lax.rem(z + d, 8)
        k, x_low, side = to // 4, lax.rem(to // 2, 2), lax.rem(to, 2)
        for x_high in range(2):
            dx = lax.rem(x - (2 * x_high + x_low) + 4, 4)
            for core in range(2):
                for goal in range(2):
                    parts = []
                    for m in range(2):
                        block = held[dx, k, m, core, goal]
                        parts.append(jnp.where(side == 0, block[:4], block[4:]))
                    outs[d][x_high * 2 + goal, core] = jnp.concatenate(parts, axis=0)
        if d % 4:
            for dy in range(4):
                outs[d][4 + dy] = direct[dy][4 + d if d < 4 else 8 - d]


def y_pack_kernel(*refs):
    came, outs, held = refs[:8], refs[8:12], refs[12]
    for d in range(8):
        held[d] = came[d][:4]
    x, y, z, c = spot()
    side = lax.rem(z, 2)
    for e in range(4):
        to = lax.rem(y + e, 4)
        z_high, x_high = to // 2, lax.rem(to, 2)
        for z_low in range(4):
            froms = []
            for m in range(2):
                low = lax.rem(x, 2) * 2 + m
                up = lax.rem(z_high * 4 + low + lax.rem(z_low - low + 4, 4), 8)
                down = lax.rem(z_high * 4 + low - lax.rem(low - z_low + 4, 4) + 8, 8)
                froms.append(lax.rem(z - jnp.where(side == 0, up, down) + 8, 8))
            for goal in range(2):
                for core in range(2):
                    a = held[froms[0], x_high * 2 + goal, core]
                    b = held[froms[1], x_high * 2 + goal, core]
                    outs[e][z_low, goal, core] = jnp.concatenate([a[:4], b[4:]], axis=0)


def swap_pack_kernel(*refs):
    c = spot()[3]
    for e in range(4):
        for z_low in range(4):
            refs[4][e, z_low] = refs[e][z_low, 1 - c]


def base_kernel(*refs):
    came, home, r_ref, base, held = refs[:6], refs[6], refs[7], refs[8], refs[9]
    x, y, z, c = spot()
    held[0] = home[0]
    held[4] = home[1]
    for n in range(3):
        held[5 + n] = came[n][4:]
        held[3 - n] = came[3 + n][4:]
    for dy in range(4):
        source = lax.rem(y - dy + 4, 4)
        for z_low in range(4):
            up = lax.rem(z_low - z + 8, 4)
            down = 4 + lax.rem(z - z_low + 4, 4)
            for core in range(2):
                v = lax.rem(c + core, 2)
                at = pl.ds(pl.multiple_of(source * 2048 + z_low * 512 + core * COLS, COLS), COLS)
                straight = jnp.concatenate([held[up, dy, v], held[down, dy, v]], axis=0)
                base[:, at] = r_ref[:, :, at].reshape(16, COLS) + straight


def final_kernel(*refs):
    mirror, swapped = refs[:4], refs[4]
    t_ref, base, pair, occupied, turn, residual, updated, moved_ref = refs[5:]
    x, y, z, c = spot()
    lane = lax.broadcasted_iota(jnp.int32, (16, 64), 1)
    row = lax.broadcasted_iota(jnp.int32, (16, 64), 0)
    i = (z // 4 * 4 + x) * 8 + row // 2
    j = ((y * 4 + lax.rem(z, 4)) * 2 + c) * 2 + row % 2
    first = jnp.sum(jnp.where(lane == i, occupied[...], 0.0), axis=1, keepdims=True)
    second = jnp.sum(jnp.where(lane == j, occupied[...], 0.0), axis=1, keepdims=True)
    order = (0, 2, 1, 3)
    for e in range(4):
        for z_low in range(4):
            for core in range(2):
                kept, given = mirror[e][z_low, c, core], swapped[e, z_low, core]
                a, b = jnp.where(c == 0, kept, given), jnp.where(c == 0, given, kept)
                rows = [s[m * 4 + n : m * 4 + n + 1] for m in range(2) for s in (a, b) for n in order]
                column = (z_low % 2 * 2 + core) * COLS
                group = e * 2 + z_low // 2
                moved_ref[group * 16 : group * 16 + 16, column : column + COLS] = jnp.concatenate(rows, axis=0)
    moved_ref[...] = exact(moved_ref[...], turn[...], (((1,), (0,)), ((), ())))
    for e in range(4):
        source = lax.rem(y - e + 4, 4)
        for half in range(2):
            group = e * 2 + half
            at = pl.ds(pl.multiple_of(source * 2048 + half * 1024, 1024), 1024)
            total = base[:, at] + moved_ref[group * 16 : group * 16 + 16, :]
            residual[:, :, at] = total.reshape(8, 2, 1024)
            ratio = total / (pair[pl.ds(source * 2 + half, 1), :] - first - second)
            updated[:, :, at] = t_ref[:, :, at] + ratio.reshape(8, 2, 1024)


VMEM = pl.BlockSpec(memory_space=pltpu.VMEM)


def shape(*dims):
    return jax.ShapeDtypeStruct(dims, F32)


def call(kernel, name, operands, outs, scratch=(), limit=8, cost=None):
    return pl.pallas_call(
        kernel,
        in_specs=[VMEM] * len(operands),
        out_specs=[VMEM] * len(outs),
        out_shape=[shape(*dims) if isinstance(dims, tuple) else dims for dims in outs],
        scratch_shapes=[pltpu.VMEM(dims, F32) for dims in scratch],
        compiler_params=pltpu.CompilerParams(vmem_limit_bytes=limit * 1024 * 1024),
        cost_estimate=cost,
        name=name,
    )(*operands)


def shards(amplitudes, residual_in, ladder_ints, occ_energy, virt_energy, virt_order):
    own, own_up, own_down = call(
        relayout_kernel, "relayout", [amplitudes], [(16, NP), (8, NP), (8, NP)]
    )
    pair_energy, turn = call(
        prepare_kernel,
        "prepare",
        [virt_order.reshape(1, NV), virt_energy.reshape(1, NV)],
        [(IRREPS, VH * VH), jax.ShapeDtypeStruct((VH * VH, VH * VH), BF16)],
        limit=16,
    )

    from_below, from_above = shift(own, dy=1), shift(own, dy=-1)
    up, down = [shift(own_up, dz=1)], [shift(own_down, dz=-1)]
    up.append(shift(up[-1], dz=1))
    down.append(shift(down[-1], dz=-1))
    far_up, far_down = shift(from_below[:8], dy=1), shift(from_above[8:], dy=-1)
    up[1], down[1], from_below, from_above = lax.optimization_barrier((up[1], down[1], from_below, from_above))
    up.append(shift(up[-1], dz=1))
    down.append(shift(down[-1], dz=-1))
    partner = shift(ladder_ints, dc=1)
    far_up, far_down, up[2], down[2] = lax.optimization_barrier((far_up, far_down, up[2], down[2]))

    (low,) = call(low_pack_kernel, "low_pack", up + down, [(48, HALF)])
    low_below, low_above = shift(low, dy=1), shift(low, dy=-1)
    low_far_up, low_far_down = shift(low_below[:24], dy=1), shift(low_above[24:], dy=-1)

    high_up, high_down = call(
        high_pack_kernel, "high_pack", [from_below, from_above, far_up, far_down], [(24, HALF)] * 2
    )
    high_ups, high_downs = [], []
    for hop in range(3):
        if hop == 1:
            mark = call(touch_kernel, "touch", [ladder_ints, partner], [(8, 128)])
            high_up, pair_energy, turn, mark = lax.optimization_barrier((high_up, pair_energy, turn, mark))
        high_up, high_down = shift(high_up, dz=1), shift(high_down, dz=-1)
        high_ups.append(high_up)
        high_downs.append(high_down)

    near = [own, from_below, from_above, far_up, far_down] + up + down
    near_slots = [slot_of(dy, side, 0) for dy in (0, 3, 1) for side in range(2)]
    near_slots += [slot_of(2, 0, 0), slot_of(2, 1, 0)]
    near_slots += [slot_of(0, side, dz) for side in range(2) for dz in (1, 2, 3)]
    low_pieces = [low_below, low_above, low_far_up, low_far_down]
    low_slots = [slot_of(dy, side, dz) for dy in (3, 1) for side in range(2) for dz in (1, 2, 3)]
    low_slots += [slot_of(2, side, dz) for side in range(2) for dz in (1, 2, 3)]
    high_pieces = high_ups + high_downs
    high_slots = [slot_of(dy, side, dz) for side in range(2) for dz in (1, 2, 3) for dy in (3, 1, 2)]

    cost = pl.CostEstimate(flops=2 * 3 * ROWS * 2 * COLS * HALF, bytes_accessed=12 << 20, transcendentals=0)
    sums = (2, 32, 8, COLS)
    total = (ROWS, 2 * COLS)
    (first,) = call(
        lambda *refs: first_half_kernel(near_slots + low_slots, *refs),
        "first_half",
        near + low_pieces + [ladder_ints, partner],
        [sums],
        [total],
        limit=MULTIPLY_LIMIT,
        cost=cost,
    )
    results = call(
        lambda *refs: second_half_kernel(near_slots + high_slots, len(near), *refs),
        "second_half",
        near + high_pieces + [ladder_ints, partner, first],
        [(8, 2, 8, COLS)] * 4 + [(2, 2, 2, 2, 8, COLS)] * 4,
        [total, sums],
        limit=MULTIPLY_LIMIT,
        cost=cost,
    )

    direct, crossed = results[:4], results[4:]
    came = [crossed[0]] + [shift(crossed[dx], dx=dx) for dx in range(1, 4)]
    direct = [direct[0]] + [shift(direct[dy], dy=dy) for dy in range(1, 4)]
    chunk, mixed = (4, 2, 8, COLS), (8, 2, 8, COLS)
    *z_sent, home = call(
        z_pack_kernel,
        "z_pack",
        came + direct,
        [mixed if d % 4 else chunk for d in range(8)] + [(2, 4, 2, 8, COLS)],
        [(4, 2, 2, 2, 2, 8, COLS)],
    )
    z_came = [z_sent[0]] + [shift(z_sent[d], dz=d) for d in range(1, 8)]
    y_sent = call(y_pack_kernel, "y_pack", z_came, [(4, 2, 2, 8, COLS)] * 4, [(8,) + chunk])
    mirror = [y_sent[0]] + [shift(y_sent[e], dy=e) for e in range(1, 4)]
    straight = [z_came[d] for d in (1, 2, 3, 5, 6, 7)]
    (base,) = call(base_kernel, "base", straight + [home, residual_in], [(16, NP)], [(8,) + chunk])
    (swapped,) = call(swap_pack_kernel, "swap_pack", mirror, [(4, 4, 2, 8, COLS)])
    swapped = shift(swapped, dc=1)
    residual, updated = call(
        final_kernel,
        "final",
        mirror + [swapped, amplitudes, base, pair_energy, occ_energy.reshape(1, 64), turn],
        [(8, 2, NP)] * 2,
        [(128, VH * VH)],
    )
    return residual, updated


def solution(mesh):
    placed = (P("ia", "ja", None), P("ia", "ja", None), P("ja", None), P(), P(), P())
    return jax.shard_map(
        shards,
        mesh=mesh,
        in_specs=placed,
        out_specs=(P("ia", "ja", None), P("ia", "ja", None)),
        check_vma=False,
    )
```

time: 221 us -> 128 us (0.58)
  waiting for transfers between devices: 136 us -> 39.7 us
  starting transfers between devices: 13.9 us -> 68.7 us
  blocking collectives: 23.8 us -> 0 us
  matrix products: 18.6 us -> 0 us
  between operations: 14.1 us -> 0.86 us
  Pallas kernels: 0 us -> 13 us
  local copies, waits for them, and re-layouts: 11.8 us -> 5.89 us
  other arithmetic: 2.24 us -> 0 us
    all_gather x1 -> x0, waiting for transfers between devices: 105 us -> none  [shards(): lax.all_gather(amplitudes, 'ja', axis=1, tiled=True)]
    ppermute x0 -> x38, starting transfers between devices: none -> 68.7 us  [shift(): return lax.ppermute(array, BOTH, moved(**steps))]
    ppermute x0 -> x38, waiting for transfers between devices: none -> 39.7 us  [shift(): return lax.ppermute(array, BOTH, moved(**steps))]
    all_to_all x2 -> x0, waiting for transfers between devices: 31.1 us -> none  [the longest x1 16 us: shards(): lax.all_to_all(mirrored, 'ja', split_axis=1, concat_axis=2, tiled=True)]
    all_to_all x1 -> x0, blocking collectives: 23.8 us -> none  [shards(): lax.all_to_all(rows, 'ia', split_axis=1, concat_axis=0, tiled=True)]
    dot_general x2 -> x0, matrix products: 18.6 us -> none  [the longest x1 18.4 us: shards(): lax.dot_general(lax.all_gather(amplitudes, 'ja', axis=1, tiled=True), lad...]
    all_to_all x2 -> x0, starting transfers between devices: 13.8 us -> none  [the longest x1 10.1 us: shards(): direct = lax.all_to_all(rows, 'ja', split_axis=1, concat_axis=2, tiled=True)]
    pallas_call x0 -> x11, Pallas kernels: none -> 13 us  [call(): pl.pallas_call(kernel, in_specs=[VMEM] * len(operands), out_specs=[VMEM]...]
  transfers between devices with their start and end apart: 3 -> 38, of which waited for: 3 -> 16; matrix products, arithmetic and copies ran while one was open for 1% -> 0% of each run, Pallas kernels for 0% -> 5%
where the time goes in v3:
time: 128 us
  starting transfers between devices  68.7 us (54%)
  waiting for transfers between devices  39.7 us (31%)
  Pallas kernels  13 us (10%)
  local copies, waits for them, and re-layouts  5.89 us (5%)
    ppermute x38, starting transfers between devices, shift(): return lax.ppermute(array, BOTH, moved(**steps))  68.7 us
    ppermute x38, waiting for transfers between devices, shift(): return lax.ppermute(array, BOTH, moved(**steps))  39.7 us
    pallas_call x11, Pallas kernels, call(): pl.pallas_call(kernel, in_specs=[VMEM] * len(operands), out_specs=[VMEM]...  13 us
    unnamed x16, local copies, waits for them, and re-layouts  5.8 us
  transfers between devices with their start and end apart: 38, of which 16 were waited for; matrix products, arithmetic and copies ran while one was open for 0% of the time, Pallas kernels for 5%

profile of v3, /device:TPU:1, one launch (start us, length us, event | category | flops | bytes accessed | tf_op | source)
XLA Modules:
  0.0 128.2 jit_solution(6355242353612089626)
XLA Ops:
  0.6 3.3 %collective-permute-start.16 = (f32[256,8192]{1,0:T(8,128)}, f32[256,8192]{1,0:T(8,128)S(1)}, u32[]{:S(2)}, u32[]{:S(2)}) collective-permute-start(f32[256,8192]{1,0:T(8,128)} %refs_17_.1), channel_id=1, source_target_pairs={{0,1},{1,0},{2,3},{3,2},{4,5},{5,4},{6,7},{7,6},{128,129},{129,128... | collective-permute-start | bytes 25165832 | tf_op jit(solution)/shard_map/ppermute | solution.py:38
  4.0 1.0 copy-done.2
  5.0 0.1 relayout.1
  5.1 0.1 collective-permute-start.4
  5.2 2.7 %collective-permute-start.5 = (f32[16,8192]{1,0:T(8,128)S(1)}, f32[16,8192]{1,0:T(8,128)S(1)}, u32[]{:S(2)}, u32[]{:S(2)}) collective-permute-start(f32[16,8192]{1,0:T(8,128)S(1)} %get-tuple-element.41.refs_0_), channel_id=1, source_target_pairs={{0,24},{1,25},{2,26},{3,27},{4,28},{5,29},{6,30},{7,31},{128,152},... | collective-permute-start | bytes 1572872 | tf_op jit(solution)/shard_map/ppermute | solution.py:38
  7.8 0.0 collective-permute-start
  7.9 3.9 %collective-permute-start.2 = (f32[8,8192]{1,0:T(8,128)S(1)}, f32[8,8192]{1,0:T(8,128)S(1)}, u32[]{:S(2)}, u32[]{:S(2)}) collective-permute-start(f32[8,8192]{1,0:T(8,128)S(1)} %get-tuple-element.43), channel_id=1, source_target_pairs={{0,134},{1,135},{2,0},{3,1},{4,2},{5,3},{6,4},{7,5},{128,6},{129,7... | collective-permute-start | bytes 786440 | tf_op jit(solution)/shard_map/ppermute | solution.py:38
  11.8 6.3 %collective-permute-done.refs_0_.refs_5_ = f32[8,8192]{1,0:T(8,128)S(1)} collective-permute-done((f32[8,8192]{1,0:T(8,128)S(1)}, f32[8,8192]{1,0:T(8,128)S(1)}, u32[]{:S(2)}, u32[]{:S(2)}) %collective-permute-start) | collective-permute-done | bytes 262176 | tf_op jit(solution)/shard_map/ppermute | solution.py:38
  18.1 2.7 %collective-permute-start.3 = (f32[8,8192]{1,0:T(8,128)S(1)}, f32[8,8192]{1,0:T(8,128)S(1)}, u32[]{:S(2)}, u32[]{:S(2)}) collective-permute-start(f32[8,8192]{1,0:T(8,128)S(1)} %collective-permute-done.2.refs_3_.refs_8_), channel_id=1, source_target_pairs={{0,134},{1,135},{2,0},{3,1},{4,2},{5,3},{6,4},{7,5},{128,6},{129,7... | collective-permute-start | bytes 786440 | tf_op jit(solution)/shard_map/ppermute | solution.py:38
  20.8 5.4 %collective-permute-done.1.refs_1_.refs_6_ = f32[8,8192]{1,0:T(8,128)S(1)} collective-permute-done((f32[8,8192]{1,0:T(8,128)S(1)}, f32[8,8192]{1,0:T(8,128)S(1)}, u32[]{:S(2)}, u32[]{:S(2)}) %collective-permute-start.1) | collective-permute-done | bytes 262176 | tf_op jit(solution)/shard_map/ppermute | solution.py:38
  26.2 2.7 %collective-permute-start.9 = (f32[8,8192]{1,0:T(8,128)S(1)}, f32[8,8192]{1,0:T(8,128)S(1)}, u32[]{:S(2)}, u32[]{:S(2)}) collective-permute-start(f32[8,8192]{1,0:T(8,128)S(1)} %collective-permute-done.3.refs_4_.refs_9_), channel_id=1, source_target_pairs={{0,134},{1,135},{2,0},{3,1},{4,2},{5,3},{6,4},{7,5},{128,6},{129,7... | collective-permute-start | bytes 786440 | tf_op jit(solution)/shard_map/ppermute | solution.py:38
  28.9 0.1 collective-permute-start.6
  29.0 2.7 %collective-permute-start.7 = (f32[8,8192]{1,0:T(8,128)S(1)}, f32[8,8192]{1,0:T(8,128)S(1)}, u32[]{:S(2)}, u32[]{:S(2)}) collective-permute-start(f32[8,8192]{1,0:T(8,128)S(1)} %slice.17), channel_id=1, source_target_pairs={{0,24},{1,25},{2,26},{3,27},{4,28},{5,29},{6,30},{7,31},{128,152},... | collective-permute-start | bytes 786440 | tf_op jit(solution)/shard_map/ppermute | solution.py:38
  31.7 1.6 %collective-permute-done.8.refs_2_.refs_7_ = f32[8,8192]{1,0:T(8,128)S(1)} collective-permute-done((f32[8,8192]{1,0:T(8,128)S(1)}, f32[8,8192]{1,0:T(8,128)S(1)}, u32[]{:S(2)}, u32[]{:S(2)}) %collective-permute-start.8) | collective-permute-done | bytes 262176 | tf_op jit(solution)/shard_map/ppermute | solution.py:38
  33.3 2.4 %collective-permute-done.6.far_up.refs_3_ = f32[8,8192]{1,0:T(8,128)S(1)} collective-permute-done((f32[8,8192]{1,0:T(8,128)S(1)}, f32[8,8192]{1,0:T(8,128)S(1)}, u32[]{:S(2)}, u32[]{:S(2)}) %collective-permute-start.6) | collective-permute-done | bytes 262176 | tf_op jit(solution)/shard_map/ppermute | solution.py:38
  35.7 0.1 low_pack.1
  35.7 0.1 collective-permute-start.17
  35.8 2.7 %collective-permute-start.18 = (f32[48,4096]{1,0:T(8,128)S(1)}, f32[48,4096]{1,0:T(8,128)S(1)}, u32[]{:S(2)}, u32[]{:S(2)}) collective-permute-start(f32[48,4096]{1,0:T(8,128)S(1)} %low_pack.1), channel_id=1, source_target_pairs={{0,24},{1,25},{2,26},{3,27},{4,28},{5,29},{6,30},{7,31},{128,152},... | collective-permute-start | bytes 2359304 | tf_op jit(solution)/shard_map/ppermute | solution.py:38
  38.5 0.1 high_pack.1
  38.5 0.1 collective-permute-start.10
  38.6 2.7 %collective-permute-start.13 = (f32[24,4096]{1,0:T(8,128)S(1)}, f32[24,4096]{1,0:T(8,128)S(1)}, u32[]{:S(2)}, u32[]{:S(2)}) collective-permute-start(f32[24,4096]{1,0:T(8,128)S(1)} %get-tuple-element.56), channel_id=1, source_target_pairs={{0,134},{1,135},{2,0},{3,1},{4,2},{5,3},{6,4},{7,5},{128,6},{129,7... | collective-permute-start | bytes 1179656 | tf_op jit(solution)/shard_map/ppermute | solution.py:38
  41.3 0.7 copy-done.5
  42.0 0.7 copy-done.6
  42.6 1.4 %prepare.1 = (f32[8,1024]{1,0:T(8,128)S(1)}, bf16[1024,1024]{1,0:T(8,128)(2,1)S(1)}) custom-call(s32[1,256]{1,0:T(1,128)S(1)} %bitcast.3, f32[1,256]{1,0:T(1,128)S(1)} %bitcast.4), custom_call_target="tpu_custom_call" | custom-call | tf_op jit(solution)/shard_map/prepare/pallas_call | solution.py:282
  44.0 2.7 %collective-permute-done.10.refs_11_ = f32[24,4096]{1,0:T(8,128)S(1)} collective-permute-done((f32[24,4096]{1,0:T(8,128)S(1)}, f32[24,4096]{1,0:T(8,128)S(1)}, u32[]{:S(2)}, u32[]{:S(2)}) %collective-permute-start.10) | collective-permute-done | bytes 393248 | tf_op jit(solution)/shard_map/ppermute | solution.py:38
  46.7 2.7 %collective-permute-start.14 = (f32[24,4096]{1,0:T(8,128)S(1)}, f32[24,4096]{1,0:T(8,128)S(1)}, u32[]{:S(2)}, u32[]{:S(2)}) collective-permute-start(f32[24,4096]{1,0:T(8,128)S(1)} %collective-permute-done.13.refs_14_), channel_id=1, source_target_pairs={{0,134},{1,135},{2,0},{3,1},{4,2},{5,3},{6,4},{7,5},{128,6},{129,7... | collective-permute-start | bytes 1179656 | tf_op jit(solution)/shard_map/ppermute | solution.py:38
  49.4 3.2 %collective-permute-done.17.refs_11_ = f32[48,4096]{1,0:T(8,128)S(1)} collective-permute-done((f32[48,4096]{1,0:T(8,128)S(1)}, f32[48,4096]{1,0:T(8,128)S(1)}, u32[]{:S(2)}, u32[]{:S(2)}) %collective-permute-start.17) | collective-permute-done | bytes 786464 | tf_op jit(solution)/shard_map/ppermute | solution.py:38
  52.7 0.1 collective-permute-start.19
  52.8 2.7 %collective-permute-start.20 = (f32[24,4096]{1,0:T(8,128)S(1)}, f32[24,4096]{1,0:T(8,128)S(1)}, u32[]{:S(2)}, u32[]{:S(2)}) collective-permute-start(f32[24,4096]{1,0:T(8,128)S(1)} %slice.19), channel_id=1, source_target_pairs={{0,24},{1,25},{2,26},{3,27},{4,28},{5,29},{6,30},{7,31},{128,152},... | collective-permute-start | bytes 1179656 | tf_op jit(solution)/shard_map/ppermute | solution.py:38
  55.5 2.7 %collective-permute-start.15 = (f32[24,4096]{1,0:T(8,128)S(1)}, f32[24,4096]{1,0:T(8,128)S(1)}, u32[]{:S(2)}, u32[]{:S(2)}) collective-permute-start(f32[24,4096]{1,0:T(8,128)S(1)} %collective-permute-done.14.refs_15_), channel_id=1, source_target_pairs={{0,134},{1,135},{2,0},{3,1},{4,2},{5,3},{6,4},{7,5},{128,6},{129,7... | collective-permute-start | bytes 1179656 | tf_op jit(solution)/shard_map/ppermute | solution.py:38
  58.2 2.7 %collective-permute-done.19.refs_13_ = f32[24,4096]{1,0:T(8,128)S(1)} collective-permute-done((f32[24,4096]{1,0:T(8,128)S(1)}, f32[24,4096]{1,0:T(8,128)S(1)}, u32[]{:S(2)}, u32[]{:S(2)}) %collective-permute-start.19) | collective-permute-done | bytes 393248 | tf_op jit(solution)/shard_map/ppermute | solution.py:38
  60.9 3.4 %copy-done = f32[256,8192]{1,0:T(8,128)S(1)} copy-done((f32[256,8192]{1,0:T(8,128)S(1)}, f32[256,8192]{1,0:T(8,128)}, u32[]{:S(2)}) %copy-start) | copy-done | bytes 8388632
  64.3 4.1 %first_half.1.refs_19_ = f32[2,32,8,256]{3,2,1,0:T(8,128)S(1)} custom-call(f32[16,8192]{1,0:T(8,128)S(1)} %get-tuple-element.41.refs_0_, f32[16,8192]{1,0:T(8,128)S(1)} %collective-permute-done.4.below.refs_1_, f32[16,8192]{1,0:T(8,128)S(1)} %collective-permute-done.5.above.refs_2_, f32[8,8192]{1,0:T(8,128)S(1)} %collective-permute-done.6.far_up.refs_3_, ...), custom_call_target="tpu_custom_call" | custom-call | flops 3221225472 | bytes 12582912 | tf_op jit(solution)/shard_map/first_half/pallas_call | solution.py:282
  68.5 4.3 %second_half.1 = (f32[8,2,8,256]{3,2,1,0:T(8,128)S(1)}, f32[8,2,8,256]{3,2,1,0:T(8,128)S(1)}, f32[8,2,8,256]{3,2,1,0:T(8,128)S(1)}, f32[8,2,8,256]{3,2,1,0:T(8,1...) custom-call(f32[16,8192]{1,0:T(8,128)S(1)} %get-tuple-element.41.ref, ...), custom_call_target="tpu_custom_call" | custom-call | flops 3221225472 | bytes 12582912 | tf_op jit(solution)/shard_map/second_half/pallas_call | solution.py:282
  72.8 1.3 %collective-permute-start.21 = (f32[2,2,2,2,8,256]{5,4,3,2,1,0:T(8,128)S(1)}, f32[2,2,2,2,8,256]{5,4,3,2,1,0:T(8,128)S(1)}, u32[]{:S(2)}, u32[]{:S(2)}) collective-permute-start(f32[2,2,2,2,8,256]{5,4,3,2,1,0:T(8,128)S(1)} %get-tuple-element.58), channel_id=1, source_target_pairs={{0,32},{1,33},{2,34},{3,35},{4,36},{5,37},{6,38},{7,39},{128,160},... | collective-permute-start | bytes 393224 | tf_op jit(solution)/shard_map/ppermute | solution.py:38
  74.1 2.4 %collective-permute-start.22 = (f32[2,2,2,2,8,256]{5,4,3,2,1,0:T(8,128)S(1)}, f32[2,2,2,2,8,256]{5,4,3,2,1,0:T(8,128)S(1)}, u32[]{:S(2)}, u32[]{:S(2)}) collective-permute-start(f32[2,2,2,2,8,256]{5,4,3,2,1,0:T(8,128)S(1)} %get-tuple-element.59), channel_id=1, source_target_pairs={{0,64},{1,65},{2,66},{3,67},{4,68},{5,69},{6,70},{7,71},{128,192},... | collective-permute-start | bytes 393224 | tf_op jit(solution)/shard_map/ppermute | solution.py:38
  76.6 1.2 collective-permute-start.23
  77.7 0.6 collective-permute-start.24
  78.3 3.4 %collective-permute-start.25 = (f32[8,2,8,256]{3,2,1,0:T(8,128)S(1)}, f32[8,2,8,256]{3,2,1,0:T(8,128)S(1)}, u32[]{:S(2)}, u32[]{:S(2)}) collective-permute-start(f32[8,2,8,256]{3,2,1,0:T(8,128)S(1)} %get-tuple-element.63), channel_id=1, source_target_pairs={{0,16},{1,17},{2,18},{3,19},{4,20},{5,21},{6,22},{7,23},{128,144},... | collective-permute-start | bytes 393224 | tf_op jit(solution)/shard_map/ppermute | solution.py:38
  81.7 0.4 collective-permute-start.26
  82.1 1.0 collective-permute-done.24.refs_5_
  83.1 2.6 %collective-permute-done.25.refs_6_ = f32[8,2,8,256]{3,2,1,0:T(8,128)S(1)} collective-permute-done((f32[8,2,8,256]{3,2,1,0:T(8,128)S(1)}, f32[8,2,8,256]{3,2,1,0:T(8,128)S(1)}, u32[]{:S(2)}, u32[]{:S(2)}) %collective-permute-start.25) | collective-permute-done | bytes 131104 | tf_op jit(solution)/shard_map/ppermute | solution.py:38
  85.7 0.1 collective-permute-done.26.refs_7_
  85.8 0.2 z_pack.1
  86.0 0.1 collective-permute-start.27
  86.1 3.0 %collective-permute-start.30 = (f32[4,2,8,256]{3,2,1,0:T(8,128)S(1)}, f32[4,2,8,256]{3,2,1,0:T(8,128)S(1)}, u32[]{:S(2)}, u32[]{:S(2)}) collective-permute-start(f32[4,2,8,256]{3,2,1,0:T(8,128)S(1)} %get-tuple-element.69), channel_id=1, source_target_pairs={{0,128},{1,129},{2,130},{3,131},{4,132},{5,133},{6,134},{7,135},{1... | collective-permute-start | bytes 196616 | tf_op jit(solution)/shard_map/ppermute | solution.py:38
  89.0 1.3 collective-permute-start.28
  90.3 1.8 %collective-permute-start.29 = (f32[8,2,8,256]{3,2,1,0:T(8,128)S(1)}, f32[8,2,8,256]{3,2,1,0:T(8,128)S(1)}, u32[]{:S(2)}, u32[]{:S(2)}) collective-permute-start(f32[8,2,8,256]{3,2,1,0:T(8,128)S(1)} %get-tuple-element.68), channel_id=1, source_target_pairs={{0,6},{1,7},{2,128},{3,129},{4,130},{5,131},{6,132},{7,133},{128,1... | collective-permute-start | bytes 393224 | tf_op jit(solution)/shard_map/ppermute | solution.py:38
  92.1 2.7 %collective-permute-start.31 = (f32[8,2,8,256]{3,2,1,0:T(8,128)S(1)}, f32[8,2,8,256]{3,2,1,0:T(8,128)S(1)}, u32[]{:S(2)}, u32[]{:S(2)}) collective-permute-start(f32[8,2,8,256]{3,2,1,0:T(8,128)S(1)} %get-tuple-element.70), channel_id=1, source_target_pairs={{0,130},{1,131},{2,132},{3,133},{4,134},{5,135},{6,0},{7,1},{128,2... | collective-permute-start | bytes 393224 | tf_op jit(solution)/shard_map/ppermute | solution.py:38
  94.8 2.3 %collective-permute-start.32 = (f32[8,2,8,256]{3,2,1,0:T(8,128)S(1)}, f32[8,2,8,256]{3,2,1,0:T(8,128)S(1)}, u32[]{:S(2)}, u32[]{:S(2)}) collective-permute-start(f32[8,2,8,256]{3,2,1,0:T(8,128)S(1)} %get-tuple-element.71), channel_id=1, source_target_pairs={{0,132},{1,133},{2,134},{3,135},{4,0},{5,1},{6,2},{7,3},{128,4},{1... | collective-permute-start | bytes 393224 | tf_op jit(solution)/shard_map/ppermute | solution.py:38
  97.1 1.4 %collective-permute-start.33 = (f32[8,2,8,256]{3,2,1,0:T(8,128)S(1)}, f32[8,2,8,256]{3,2,1,0:T(8,128)S(1)}, u32[]{:S(2)}, u32[]{:S(2)}) collective-permute-start(f32[8,2,8,256]{3,2,1,0:T(8,128)S(1)} %get-tuple-element.72), channel_id=1, source_target_pairs={{0,134},{1,135},{2,0},{3,1},{4,2},{5,3},{6,4},{7,5},{128,6},{129,7... | collective-permute-start | bytes 393224 | tf_op jit(solution)/shard_map/ppermute | solution.py:38
  98.5 5.8 %collective-permute-done.29.refs_3_.refs_2_ = f32[8,2,8,256]{3,2,1,0:T(8,128)S(1)} collective-permute-done((f32[8,2,8,256]{3,2,1,0:T(8,128)S(1)}, f32[8,2,8,256]{3,2,1,0:T(8,128)S(1)}, u32[]{:S(2)}, u32[]{:S(2)}) %collective-permute-start.29) | collective-permute-done | bytes 131104 | tf_op jit(solution)/shard_map/ppermute | solution.py:38
  104.3 2.2 %collective-permute-done.33.refs_7_.refs_5_ = f32[8,2,8,256]{3,2,1,0:T(8,128)S(1)} collective-permute-done((f32[8,2,8,256]{3,2,1,0:T(8,128)S(1)}, f32[8,2,8,256]{3,2,1,0:T(8,128)S(1)}, u32[]{:S(2)}, u32[]{:S(2)}) %collective-permute-start.33) | collective-permute-done | bytes 131104 | tf_op jit(solution)/shard_map/ppermute | solution.py:38
  106.5 0.3 y_pack.1
  106.8 0.5 collective-permute-start.34
  107.4 2.6 %collective-permute-start.35 = (f32[4,2,2,8,256]{4,3,2,1,0:T(8,128)S(1)}, f32[4,2,2,8,256]{4,3,2,1,0:T(8,128)S(1)}, u32[]{:S(2)}, u32[]{:S(2)}) collective-permute-start(f32[4,2,2,8,256]{4,3,2,1,0:T(8,128)S(1)} %get-tuple-element.75), channel_id=1, source_target_pairs={{0,16},{1,17},{2,18},{3,19},{4,20},{5,21},{6,22},{7,23},{128,144},... | collective-permute-start | bytes 393224 | tf_op jit(solution)/shard_map/ppermute | solution.py:38
  110.0 1.3 %collective-permute-start.36 = (f32[4,2,2,8,256]{4,3,2,1,0:T(8,128)S(1)}, f32[4,2,2,8,256]{4,3,2,1,0:T(8,128)S(1)}, u32[]{:S(2)}, u32[]{:S(2)}) collective-permute-start(f32[4,2,2,8,256]{4,3,2,1,0:T(8,128)S(1)} %get-tuple-element.76), channel_id=1, source_target_pairs={{0,24},{1,25},{2,26},{3,27},{4,28},{5,29},{6,30},{7,31},{128,152},... | collective-permute-start | bytes 393224 | tf_op jit(solution)/shard_map/ppermute | solution.py:38
  111.3 0.9 collective-permute-done.34.refs_1_
  112.2 1.6 %collective-permute-done.35.refs_2_ = f32[4,2,2,8,256]{4,3,2,1,0:T(8,128)S(1)} collective-permute-done((f32[4,2,2,8,256]{4,3,2,1,0:T(8,128)S(1)}, f32[4,2,2,8,256]{4,3,2,1,0:T(8,128)S(1)}, u32[]{:S(2)}, u32[]{:S(2)}) %collective-permute-start.35) | collective-permute-done | bytes 131104 | tf_op jit(solution)/shard_map/ppermute | solution.py:38
  113.7 0.5 collective-permute-done.36.refs_3_
  114.2 10.6 %collective-permute-start.37 = (f32[4,4,2,8,256]{4,3,2,1,0:T(8,128)S(1)}, f32[4,4,2,8,256]{4,3,2,1,0:T(8,128)S(1)}, u32[]{:S(2)}, u32[]{:S(2)}) collective-permute-start(f32[4,4,2,8,256]{4,3,2,1,0:T(8,128)S(1)} %swap_pack.1), channel_id=1, source_target_pairs={{0,1},{1,0},{2,3},{3,2},{4,5},{5,4},{6,7},{7,6},{128,129},{129,128... | collective-permute-start | bytes 786440 | tf_op jit(solution)/shard_map/ppermute | solution.py:38
  124.8 0.2 base.1.refs_6_
  125.0 0.9 collective-permute-done.37.refs_4_
  126.0 2.2 %final.1 = (f32[8,2,8192]{2,1,0:T(2,128)}, f32[8,2,8192]{2,1,0:T(2,128)}) custom-call(f32[4,2,2,8,256]{4,3,2,1,0:T(8,128)S(1)} %get-tuple-element.73.refs_0_, f32[4,2,2,8,256]{4,3,2,1,0:T(8,128)S(1)} %collective-permute-done.34.refs_1_, f32[4,2,2,8,256]{4,3,2,1,0:T(8,128)S(1)} %collective-permute-done.35.refs_2_, ...), custom_call_target="tpu_custom_call" | custom-call | tf_op jit(solution)/shard_map/final/pallas_call | solution.py:282
  (43 shorter events, 0.2 us)
Async XLA Ops:
  0.6 60.3 %collective-permute-start.16 = (f32[256,8192]{1,0:T(8,128)}, f32[256,8192]{1,0:T(8,128)S(1)}, u32[]{:S(2)}, u32[]{:S(2)}) collective-permute-start(f32[256,8192]{1,0:T(8,128)} %refs_17_.1), channel_id=1, source_target_pairs={{0,1},{1,0},{2,3},{3,2},{4,5},{5,4},{6,7},{7,6},{128,129},{129,128... | collective-permute-start | bytes 25165832 | tf_op jit(solution)/shard_map/ppermute | solution.py:38
  4.0 1.0 copy-start.2
  5.1 15.7 %collective-permute-start.4 = (f32[16,8192]{1,0:T(8,128)S(1)}, f32[16,8192]{1,0:T(8,128)S(1)}, u32[]{:S(2)}, u32[]{:S(2)}) collective-permute-start(f32[16,8192]{1,0:T(8,128)S(1)} %get-tuple-element.41.refs_0_), channel_id=1, source_target_pairs={{0,8},{1,9},{2,10},{3,11},{4,12},{5,13},{6,14},{7,15},{128,136},{1... | collective-permute-start | bytes 1572872 | tf_op jit(solution)/shard_map/ppermute | solution.py:38
  5.2 15.6 %collective-permute-start.5 = (f32[16,8192]{1,0:T(8,128)S(1)}, f32[16,8192]{1,0:T(8,128)S(1)}, u32[]{:S(2)}, u32[]{:S(2)}) collective-permute-start(f32[16,8192]{1,0:T(8,128)S(1)} %get-tuple-element.41.refs_0_), channel_id=1, source_target_pairs={{0,24},{1,25},{2,26},{3,27},{4,28},{5,29},{6,30},{7,31},{128,152},... | collective-permute-start | bytes 1572872 | tf_op jit(solution)/shard_map/ppermute | solution.py:38
  7.8 10.3 %collective-permute-start = (f32[8,8192]{1,0:T(8,128)S(1)}, f32[8,8192]{1,0:T(8,128)S(1)}, u32[]{:S(2)}, u32[]{:S(2)}) collective-permute-start(f32[8,8192]{1,0:T(8,128)S(1)} %get-tuple-element.42), channel_id=1, source_target_pairs={{0,2},{1,3},{2,4},{3,5},{4,6},{5,7},{6,128},{7,129},{128,130},{129... | collective-permute-start | bytes 786440 | tf_op jit(solution)/shard_map/ppermute | solution.py:38
  7.9 10.2 %collective-permute-start.2 = (f32[8,8192]{1,0:T(8,128)S(1)}, f32[8,8192]{1,0:T(8,128)S(1)}, u32[]{:S(2)}, u32[]{:S(2)}) collective-permute-start(f32[8,8192]{1,0:T(8,128)S(1)} %get-tuple-element.43), channel_id=1, source_target_pairs={{0,134},{1,135},{2,0},{3,1},{4,2},{5,3},{6,4},{7,5},{128,6},{129,7... | collective-permute-start | bytes 786440 | tf_op jit(solution)/shard_map/ppermute | solution.py:38
  18.1 8.0 %collective-permute-start.1 = (f32[8,8192]{1,0:T(8,128)S(1)}, f32[8,8192]{1,0:T(8,128)S(1)}, u32[]{:S(2)}, u32[]{:S(2)}) collective-permute-start(f32[8,8192]{1,0:T(8,128)S(1)} %collective-permute-done.refs_0_.refs_5_), channel_id=1, source_target_pairs={{0,2},{1,3},{2,4},{3,5},{4,6},{5,7},{6,128},{7,129},{128,130},{129... | collective-permute-start | bytes 786440 | tf_op jit(solution)/shard_map/ppermute | solution.py:38
  18.1 8.0 %collective-permute-start.3 = (f32[8,8192]{1,0:T(8,128)S(1)}, f32[8,8192]{1,0:T(8,128)S(1)}, u32[]{:S(2)}, u32[]{:S(2)}) collective-permute-start(f32[8,8192]{1,0:T(8,128)S(1)} %collective-permute-done.2.refs_3_.refs_8_), channel_id=1, source_target_pairs={{0,134},{1,135},{2,0},{3,1},{4,2},{5,3},{6,4},{7,5},{128,6},{129,7... | collective-permute-start | bytes 786440 | tf_op jit(solution)/shard_map/ppermute | solution.py:38
  26.2 7.1 %collective-permute-start.8 = (f32[8,8192]{1,0:T(8,128)S(1)}, f32[8,8192]{1,0:T(8,128)S(1)}, u32[]{:S(2)}, u32[]{:S(2)}) collective-permute-start(f32[8,8192]{1,0:T(8,128)S(1)} %collective-permute-done.1.refs_1_.refs_6_), channel_id=1, source_target_pairs={{0,2},{1,3},{2,4},{3,5},{4,6},{5,7},{6,128},{7,129},{128,130},{129... | collective-permute-start | bytes 786440 | tf_op jit(solution)/shard_map/ppermute | solution.py:38
  26.2 7.1 %collective-permute-start.9 = (f32[8,8192]{1,0:T(8,128)S(1)}, f32[8,8192]{1,0:T(8,128)S(1)}, u32[]{:S(2)}, u32[]{:S(2)}) collective-permute-start(f32[8,8192]{1,0:T(8,128)S(1)} %collective-permute-done.3.refs_4_.refs_9_), channel_id=1, source_target_pairs={{0,134},{1,135},{2,0},{3,1},{4,2},{5,3},{6,4},{7,5},{128,6},{129,7... | collective-permute-start | bytes 786440 | tf_op jit(solution)/shard_map/ppermute | solution.py:38
  28.9 6.8 %collective-permute-start.6 = (f32[8,8192]{1,0:T(8,128)S(1)}, f32[8,8192]{1,0:T(8,128)S(1)}, u32[]{:S(2)}, u32[]{:S(2)}) collective-permute-start(f32[8,8192]{1,0:T(8,128)S(1)} %slice.16), channel_id=1, source_target_pairs={{0,8},{1,9},{2,10},{3,11},{4,12},{5,13},{6,14},{7,15},{128,136},{1... | collective-permute-start | bytes 786440 | tf_op jit(solution)/shard_map/ppermute | solution.py:38
  29.0 6.7 %collective-permute-start.7 = (f32[8,8192]{1,0:T(8,128)S(1)}, f32[8,8192]{1,0:T(8,128)S(1)}, u32[]{:S(2)}, u32[]{:S(2)}) collective-permute-start(f32[8,8192]{1,0:T(8,128)S(1)} %slice.17), channel_id=1, source_target_pairs={{0,24},{1,25},{2,26},{3,27},{4,28},{5,29},{6,30},{7,31},{128,152},... | collective-permute-start | bytes 786440 | tf_op jit(solution)/shard_map/ppermute | solution.py:38
  35.7 16.9 %collective-permute-start.17 = (f32[48,4096]{1,0:T(8,128)S(1)}, f32[48,4096]{1,0:T(8,128)S(1)}, u32[]{:S(2)}, u32[]{:S(2)}) collective-permute-start(f32[48,4096]{1,0:T(8,128)S(1)} %low_pack.1), channel_id=1, source_target_pairs={{0,8},{1,9},{2,10},{3,11},{4,12},{5,13},{6,14},{7,15},{128,136},{1... | collective-permute-start | bytes 2359304 | tf_op jit(solution)/shard_map/ppermute | solution.py:38
  35.8 17.0 %collective-permute-start.18 = (f32[48,4096]{1,0:T(8,128)S(1)}, f32[48,4096]{1,0:T(8,128)S(1)}, u32[]{:S(2)}, u32[]{:S(2)}) collective-permute-start(f32[48,4096]{1,0:T(8,128)S(1)} %low_pack.1), channel_id=1, source_target_pairs={{0,24},{1,25},{2,26},{3,27},{4,28},{5,29},{6,30},{7,31},{128,152},... | collective-permute-start | bytes 2359304 | tf_op jit(solution)/shard_map/ppermute | solution.py:38
  38.5 8.2 %collective-permute-start.10 = (f32[24,4096]{1,0:T(8,128)S(1)}, f32[24,4096]{1,0:T(8,128)S(1)}, u32[]{:S(2)}, u32[]{:S(2)}) collective-permute-start(f32[24,4096]{1,0:T(8,128)S(1)} %get-tuple-element.52), channel_id=1, source_target_pairs={{0,2},{1,3},{2,4},{3,5},{4,6},{5,7},{6,128},{7,129},{128,130},{129... | collective-permute-start | bytes 1179656 | tf_op jit(solution)/shard_map/ppermute | solution.py:38
  38.6 8.1 %collective-permute-start.13 = (f32[24,4096]{1,0:T(8,128)S(1)}, f32[24,4096]{1,0:T(8,128)S(1)}, u32[]{:S(2)}, u32[]{:S(2)}) collective-permute-start(f32[24,4096]{1,0:T(8,128)S(1)} %get-tuple-element.56), channel_id=1, source_target_pairs={{0,134},{1,135},{2,0},{3,1},{4,2},{5,3},{6,4},{7,5},{128,6},{129,7... | collective-permute-start | bytes 1179656 | tf_op jit(solution)/shard_map/ppermute | solution.py:38
  41.3 0.7 copy-start.5
  42.0 0.7 copy-start.6
  46.7 8.8 %collective-permute-start.11 = (f32[24,4096]{1,0:T(8,128)S(1)}, f32[24,4096]{1,0:T(8,128)S(1)}, u32[]{:S(2)}, u32[]{:S(2)}) collective-permute-start(f32[24,4096]{1,0:T(8,128)S(1)} %collective-permute-done.10.refs_11_), channel_id=1, source_target_pairs={{0,2},{1,3},{2,4},{3,5},{4,6},{5,7},{6,128},{7,129},{128,130},{129... | collective-permute-start | bytes 1179656 | tf_op jit(solution)/shard_map/ppermute | solution.py:38
  46.7 8.8 %collective-permute-start.14 = (f32[24,4096]{1,0:T(8,128)S(1)}, f32[24,4096]{1,0:T(8,128)S(1)}, u32[]{:S(2)}, u32[]{:S(2)}) collective-permute-start(f32[24,4096]{1,0:T(8,128)S(1)} %collective-permute-done.13.refs_14_), channel_id=1, source_target_pairs={{0,134},{1,135},{2,0},{3,1},{4,2},{5,3},{6,4},{7,5},{128,6},{129,7... | collective-permute-start | bytes 1179656 | tf_op jit(solution)/shard_map/ppermute | solution.py:38
  52.7 8.2 %collective-permute-start.19 = (f32[24,4096]{1,0:T(8,128)S(1)}, f32[24,4096]{1,0:T(8,128)S(1)}, u32[]{:S(2)}, u32[]{:S(2)}) collective-permute-start(f32[24,4096]{1,0:T(8,128)S(1)} %slice.18), channel_id=1, source_target_pairs={{0,8},{1,9},{2,10},{3,11},{4,12},{5,13},{6,14},{7,15},{128,136},{1... | collective-permute-start | bytes 1179656 | tf_op jit(solution)/shard_map/ppermute | solution.py:38
  52.8 8.1 %collective-permute-start.20 = (f32[24,4096]{1,0:T(8,128)S(1)}, f32[24,4096]{1,0:T(8,128)S(1)}, u32[]{:S(2)}, u32[]{:S(2)}) collective-permute-start(f32[24,4096]{1,0:T(8,128)S(1)} %slice.19), channel_id=1, source_target_pairs={{0,24},{1,25},{2,26},{3,27},{4,28},{5,29},{6,30},{7,31},{128,152},... | collective-permute-start | bytes 1179656 | tf_op jit(solution)/shard_map/ppermute | solution.py:38
  55.5 12.9 %collective-permute-start.12 = (f32[24,4096]{1,0:T(8,128)S(1)}, f32[24,4096]{1,0:T(8,128)S(1)}, u32[]{:S(2)}, u32[]{:S(2)}) collective-permute-start(f32[24,4096]{1,0:T(8,128)S(1)} %collective-permute-done.11.refs_12_), channel_id=1, source_target_pairs={{0,2},{1,3},{2,4},{3,5},{4,6},{5,7},{6,128},{7,129},{128,130},{129... | collective-permute-start | bytes 1179656 | tf_op jit(solution)/shard_map/ppermute | solution.py:38
  55.5 12.9 %collective-permute-start.15 = (f32[24,4096]{1,0:T(8,128)S(1)}, f32[24,4096]{1,0:T(8,128)S(1)}, u32[]{:S(2)}, u32[]{:S(2)}) collective-permute-start(f32[24,4096]{1,0:T(8,128)S(1)} %collective-permute-done.14.refs_15_), channel_id=1, source_target_pairs={{0,134},{1,135},{2,0},{3,1},{4,2},{5,3},{6,4},{7,5},{128,6},{129,7... | collective-permute-start | bytes 1179656 | tf_op jit(solution)/shard_map/ppermute | solution.py:38
  60.9 3.4 %copy-start = (f32[256,8192]{1,0:T(8,128)S(1)}, f32[256,8192]{1,0:T(8,128)}, u32[]{:S(2)}) copy-start(f32[256,8192]{1,0:T(8,128)} %refs_17_.1) | copy-start | bytes 25165828
  64.3 4.2 %copy-start.1 = (f32[256,8192]{1,0:T(8,128)S(1)}, f32[256,8192]{1,0:T(8,128)}, u32[]{:S(2)}) copy-start(f32[256,8192]{1,0:T(8,128)} %refs_17_.1) | copy-start | bytes 25165828
  68.4 56.4 %copy-start.4 = (f32[8,2,8192]{2,1,0:T(2,128)S(1)}, f32[8,2,8192]{2,1,0:T(2,128)}, u32[]{:S(2)}) copy-start(f32[8,2,8192]{2,1,0:T(2,128)} %refs_7_.1) | copy-start | bytes 1572868
  68.4 57.5 %copy-start.3 = (f32[8,2,8192]{2,1,0:T(2,128)S(1)}, f32[8,2,8192]{2,1,0:T(2,128)}, u32[]{:S(2)}) copy-start(f32[8,2,8192]{2,1,0:T(2,128)} %refs_5_.1) | copy-start | bytes 1572868
  68.4 57.5 %copy-start.7 = (f32[64]{0:T(128)S(1)}, f32[64]{0:T(128)}, u32[]{:S(2)}) copy-start(f32[64]{0:T(128)} %param.9) | copy-start | bytes 772
  72.8 8.9 %collective-permute-start.21 = (f32[2,2,2,2,8,256]{5,4,3,2,1,0:T(8,128)S(1)}, f32[2,2,2,2,8,256]{5,4,3,2,1,0:T(8,128)S(1)}, u32[]{:S(2)}, u32[]{:S(2)}) collective-permute-start(f32[2,2,2,2,8,256]{5,4,3,2,1,0:T(8,128)S(1)} %get-tuple-element.58), channel_id=1, source_target_pairs={{0,32},{1,33},{2,34},{3,35},{4,36},{5,37},{6,38},{7,39},{128,160},... | collective-permute-start | bytes 393224 | tf_op jit(solution)/shard_map/ppermute | solution.py:38
  74.1 8.0 %collective-permute-start.22 = (f32[2,2,2,2,8,256]{5,4,3,2,1,0:T(8,128)S(1)}, f32[2,2,2,2,8,256]{5,4,3,2,1,0:T(8,128)S(1)}, u32[]{:S(2)}, u32[]{:S(2)}) collective-permute-start(f32[2,2,2,2,8,256]{5,4,3,2,1,0:T(8,128)S(1)} %get-tuple-element.59), channel_id=1, source_target_pairs={{0,64},{1,65},{2,66},{3,67},{4,68},{5,69},{6,70},{7,71},{128,192},... | collective-permute-start | bytes 393224 | tf_op jit(solution)/shard_map/ppermute | solution.py:38
  76.6 5.6 %collective-permute-start.23 = (f32[2,2,2,2,8,256]{5,4,3,2,1,0:T(8,128)S(1)}, f32[2,2,2,2,8,256]{5,4,3,2,1,0:T(8,128)S(1)}, u32[]{:S(2)}, u32[]{:S(2)}) collective-permute-start(f32[2,2,2,2,8,256]{5,4,3,2,1,0:T(8,128)S(1)} %get-tuple-element.60), channel_id=1, source_target_pairs={{0,96},{1,97},{2,98},{3,99},{4,100},{5,101},{6,102},{7,103},{128,2... | collective-permute-start | bytes 393224 | tf_op jit(solution)/shard_map/ppermute | solution.py:38
  77.7 5.4 %collective-permute-start.24 = (f32[8,2,8,256]{3,2,1,0:T(8,128)S(1)}, f32[8,2,8,256]{3,2,1,0:T(8,128)S(1)}, u32[]{:S(2)}, u32[]{:S(2)}) collective-permute-start(f32[8,2,8,256]{3,2,1,0:T(8,128)S(1)} %get-tuple-element.62), channel_id=1, source_target_pairs={{0,8},{1,9},{2,10},{3,11},{4,12},{5,13},{6,14},{7,15},{128,136},{1... | collective-permute-start | bytes 393224 | tf_op jit(solution)/shard_map/ppermute | solution.py:38
  78.3 7.5 %collective-permute-start.25 = (f32[8,2,8,256]{3,2,1,0:T(8,128)S(1)}, f32[8,2,8,256]{3,2,1,0:T(8,128)S(1)}, u32[]{:S(2)}, u32[]{:S(2)}) collective-permute-start(f32[8,2,8,256]{3,2,1,0:T(8,128)S(1)} %get-tuple-element.63), channel_id=1, source_target_pairs={{0,16},{1,17},{2,18},{3,19},{4,20},{5,21},{6,22},{7,23},{128,144},... | collective-permute-start | bytes 393224 | tf_op jit(solution)/shard_map/ppermute | solution.py:38
  81.7 4.1 %collective-permute-start.26 = (f32[8,2,8,256]{3,2,1,0:T(8,128)S(1)}, f32[8,2,8,256]{3,2,1,0:T(8,128)S(1)}, u32[]{:S(2)}, u32[]{:S(2)}) collective-permute-start(f32[8,2,8,256]{3,2,1,0:T(8,128)S(1)} %get-tuple-element.64), channel_id=1, source_target_pairs={{0,24},{1,25},{2,26},{3,27},{4,28},{5,29},{6,30},{7,31},{128,152},... | collective-permute-start | bytes 393224 | tf_op jit(solution)/shard_map/ppermute | solution.py:38
  86.0 11.1 %collective-permute-start.27 = (f32[8,2,8,256]{3,2,1,0:T(8,128)S(1)}, f32[8,2,8,256]{3,2,1,0:T(8,128)S(1)}, u32[]{:S(2)}, u32[]{:S(2)}) collective-permute-start(f32[8,2,8,256]{3,2,1,0:T(8,128)S(1)} %get-tuple-element.66), channel_id=1, source_target_pairs={{0,2},{1,3},{2,4},{3,5},{4,6},{5,7},{6,128},{7,129},{128,130},{129... | collective-permute-start | bytes 393224 | tf_op jit(solution)/shard_map/ppermute | solution.py:38
  86.1 8.7 %collective-permute-start.30 = (f32[4,2,8,256]{3,2,1,0:T(8,128)S(1)}, f32[4,2,8,256]{3,2,1,0:T(8,128)S(1)}, u32[]{:S(2)}, u32[]{:S(2)}) collective-permute-start(f32[4,2,8,256]{3,2,1,0:T(8,128)S(1)} %get-tuple-element.69), channel_id=1, source_target_pairs={{0,128},{1,129},{2,130},{3,131},{4,132},{5,133},{6,134},{7,135},{1... | collective-permute-start | bytes 196616 | tf_op jit(solution)/shard_map/ppermute | solution.py:38
  89.0 9.4 %collective-permute-start.28 = (f32[8,2,8,256]{3,2,1,0:T(8,128)S(1)}, f32[8,2,8,256]{3,2,1,0:T(8,128)S(1)}, u32[]{:S(2)}, u32[]{:S(2)}) collective-permute-start(f32[8,2,8,256]{3,2,1,0:T(8,128)S(1)} %get-tuple-element.67), channel_id=1, source_target_pairs={{0,4},{1,5},{2,6},{3,7},{4,128},{5,129},{6,130},{7,131},{128,132},... | collective-permute-start | bytes 393224 | tf_op jit(solution)/shard_map/ppermute | solution.py:38
  90.3 14.0 %collective-permute-start.29 = (f32[8,2,8,256]{3,2,1,0:T(8,128)S(1)}, f32[8,2,8,256]{3,2,1,0:T(8,128)S(1)}, u32[]{:S(2)}, u32[]{:S(2)}) collective-permute-start(f32[8,2,8,256]{3,2,1,0:T(8,128)S(1)} %get-tuple-element.68), channel_id=1, source_target_pairs={{0,6},{1,7},{2,128},{3,129},{4,130},{5,131},{6,132},{7,133},{128,1... | collective-permute-start | bytes 393224 | tf_op jit(solution)/shard_map/ppermute | solution.py:38
  92.1 12.2 %collective-permute-start.31 = (f32[8,2,8,256]{3,2,1,0:T(8,128)S(1)}, f32[8,2,8,256]{3,2,1,0:T(8,128)S(1)}, u32[]{:S(2)}, u32[]{:S(2)}) collective-permute-start(f32[8,2,8,256]{3,2,1,0:T(8,128)S(1)} %get-tuple-element.70), channel_id=1, source_target_pairs={{0,130},{1,131},{2,132},{3,133},{4,134},{5,135},{6,0},{7,1},{128,2... | collective-permute-start | bytes 393224 | tf_op jit(solution)/shard_map/ppermute | solution.py:38
  94.8 9.5 %collective-permute-start.32 = (f32[8,2,8,256]{3,2,1,0:T(8,128)S(1)}, f32[8,2,8,256]{3,2,1,0:T(8,128)S(1)}, u32[]{:S(2)}, u32[]{:S(2)}) collective-permute-start(f32[8,2,8,256]{3,2,1,0:T(8,128)S(1)} %get-tuple-element.71), channel_id=1, source_target_pairs={{0,132},{1,133},{2,134},{3,135},{4,0},{5,1},{6,2},{7,3},{128,4},{1... | collective-permute-start | bytes 393224 | tf_op jit(solution)/shard_map/ppermute | solution.py:38
  97.1 9.4 %collective-permute-start.33 = (f32[8,2,8,256]{3,2,1,0:T(8,128)S(1)}, f32[8,2,8,256]{3,2,1,0:T(8,128)S(1)}, u32[]{:S(2)}, u32[]{:S(2)}) collective-permute-start(f32[8,2,8,256]{3,2,1,0:T(8,128)S(1)} %get-tuple-element.72), channel_id=1, source_target_pairs={{0,134},{1,135},{2,0},{3,1},{4,2},{5,3},{6,4},{7,5},{128,6},{129,7... | collective-permute-start | bytes 393224 | tf_op jit(solution)/shard_map/ppermute | solution.py:38
  106.8 5.4 %collective-permute-start.34 = (f32[4,2,2,8,256]{4,3,2,1,0:T(8,128)S(1)}, f32[4,2,2,8,256]{4,3,2,1,0:T(8,128)S(1)}, u32[]{:S(2)}, u32[]{:S(2)}) collective-permute-start(f32[4,2,2,8,256]{4,3,2,1,0:T(8,128)S(1)} %get-tuple-element.74), channel_id=1, source_target_pairs={{0,8},{1,9},{2,10},{3,11},{4,12},{5,13},{6,14},{7,15},{128,136},{1... | collective-permute-start | bytes 393224 | tf_op jit(solution)/shard_map/ppermute | solution.py:38
  107.4 6.4 %collective-permute-start.35 = (f32[4,2,2,8,256]{4,3,2,1,0:T(8,128)S(1)}, f32[4,2,2,8,256]{4,3,2,1,0:T(8,128)S(1)}, u32[]{:S(2)}, u32[]{:S(2)}) collective-permute-start(f32[4,2,2,8,256]{4,3,2,1,0:T(8,128)S(1)} %get-tuple-element.75), channel_id=1, source_target_pairs={{0,16},{1,17},{2,18},{3,19},{4,20},{5,21},{6,22},{7,23},{128,144},... | collective-permute-start | bytes 393224 | tf_op jit(solution)/shard_map/ppermute | solution.py:38
  110.0 4.2 %collective-permute-start.36 = (f32[4,2,2,8,256]{4,3,2,1,0:T(8,128)S(1)}, f32[4,2,2,8,256]{4,3,2,1,0:T(8,128)S(1)}, u32[]{:S(2)}, u32[]{:S(2)}) collective-permute-start(f32[4,2,2,8,256]{4,3,2,1,0:T(8,128)S(1)} %get-tuple-element.76), channel_id=1, source_target_pairs={{0,24},{1,25},{2,26},{3,27},{4,28},{5,29},{6,30},{7,31},{128,152},... | collective-permute-start | bytes 393224 | tf_op jit(solution)/shard_map/ppermute | solution.py:38
  114.2 11.7 %collective-permute-start.37 = (f32[4,4,2,8,256]{4,3,2,1,0:T(8,128)S(1)}, f32[4,4,2,8,256]{4,3,2,1,0:T(8,128)S(1)}, u32[]{:S(2)}, u32[]{:S(2)}) collective-permute-start(f32[4,4,2,8,256]{4,3,2,1,0:T(8,128)S(1)} %swap_pack.1), channel_id=1, source_target_pairs={{0,1},{1,0},{2,3},{3,2},{4,5},{5,4},{6,7},{7,6},{128,129},{129,128... | collective-permute-start | bytes 786440 | tf_op jit(solution)/shard_map/ppermute | solution.py:38
